TPU v7x, 128 devices: a whole 4x4x4 slice. The times are simulated.
128 devices in a mesh: seq: 2 (over y_lo), fsdp: 64 (over z, y_hi, x, core).
Axes of the slice: x: 4, y: 4 (y_hi: 2, y_lo: 2; y = y_hi * 2 + y_lo), z: 4, core: 2. Of those that a mesh axis runs over, the one named last changes fastest.
Arguments:
- inputs: bfloat16 [64, 256, 1536], P('fsdp', 'seq'), may hold values from -6 to 6
- cotangent: bfloat16 [64, 256, 1536], P('fsdp', 'seq'), may hold values from -6 to 6
- attn_weight: float32 [1536, 3584], P('fsdp'), may hold values from -4 to 4
- attn_moment_one: float32 [1536, 3584], P('fsdp'), may hold values from -16384 to 16384
- attn_moment_two: float32 [1536, 3584], P('fsdp'), may hold values from 0 to 262144, as said below
- mlp_weight: float32 [1536, 26880], P('fsdp'), may hold values from -4 to 4
- mlp_moment_one: float32 [1536, 26880], P('fsdp'), may hold values from -16384 to 16384
- mlp_moment_two: float32 [1536, 26880], P('fsdp'), may hold values from 0 to 262144, as said below
- vectors: float32 [5120], P('fsdp'), may hold values from -2 to 2, as said below
- vector_moment_one: float32 [5120], P('fsdp'), may hold values from -16384 to 16384
- vector_moment_two: float32 [5120], P('fsdp'), may hold values from 0 to 262144, as said below
Outputs:
- output: bfloat16 [64, 256, 1536], P('fsdp', 'seq')
- input_grad: float32 [64, 256, 1536], P('fsdp', 'seq')
- attn_moment_one_new: float32 [1536, 3584], P('fsdp')
- attn_moment_two_new: float32 [1536, 3584], P('fsdp')
- attn_weight_new: float32 [1536, 3584], P('fsdp')
- mlp_moment_one_new: float32 [1536, 26880], P('fsdp')
- mlp_moment_two_new: float32 [1536, 26880], P('fsdp')
- mlp_weight_new: float32 [1536, 26880], P('fsdp')
- vector_moment_one_new: float32 [5120], P('fsdp')
- vector_moment_two_new: float32 [5120], P('fsdp')
- vectors_new: float32 [5120], P('fsdp')
Inputs may be any that keep to these rules, and one draw needn't show every extreme that they name: `attn_moment_two`: positive. `mlp_moment_two`: positive. `vectors`: gains lie in 0.6 to 1.4. `vector_moment_two`: positive.
All inputs are finite; a program needn't handle non-finite values.
Results may differ from a plain program's by a relative error of at most 0.018.
Values may be sent and summed in bfloat16 or wider, within the bound.
No kernel may reach another device: no remote copies, remote signals or barrier semaphores. Data moves between devices by JAX's collectives and lax.ppermute only.
A program may use at most 832 MiB of HBM per device.

v0:
```python
import jax
import jax.numpy as jnp
from jax import lax
from jax.sharding import PartitionSpec as P

D = 1536
H = 12
KV = 2
HD = 128
FF = 8960
STEP = 10
QKV = 2048


norm_eps = 1e-06
rope_base = 1000000.0


def rotary_tables(row_start, row_count):
    half_dim = HD // 2
    freqs = rope_base ** (-jnp.arange(half_dim, dtype=jnp.float32) * 2.0 / HD)
    places = (row_start + jnp.arange(row_count)).astype(jnp.float32)
    angles = places[:, None] * freqs[None, :]
    angles = jnp.concatenate([angles, angles], axis=1)
    return (jnp.cos(angles), jnp.sin(angles))


def rotate(values, cos_table, sin_table):
    half_dim = values.shape[-1] // 2
    turned = jnp.concatenate([-values[..., half_dim:], values[..., :half_dim]], axis=-1)
    return values * cos_table[:, None, :] + turned * sin_table[:, None, :]


def unrotate(values, cos_table, sin_table):
    half_dim = values.shape[-1] // 2
    moved_sine = values * sin_table[:, None, :]
    turned = jnp.concatenate([moved_sine[..., half_dim:], -moved_sine[..., :half_dim]], axis=-1)
    return values * cos_table[:, None, :] + turned


def adam_update(weight, moment_one, moment_two, gradient, step_rate):
    moment_one = 0.9 * moment_one + 0.1 * gradient
    moment_two = 0.95 * moment_two + 0.05 * gradient * gradient
    first_hat = moment_one / (1.0 - 0.9**STEP)
    second_hat = moment_two / (1.0 - 0.95**STEP)
    updated = weight - step_rate * (first_hat / (jnp.sqrt(second_hat) + 1e-08) + 0.1 * weight)
    return (moment_one, moment_two, updated)


def shards(
    inputs,
    cotangent,
    attn_weight,
    attn_moment_one,
    attn_moment_two,
    mlp_weight,
    mlp_moment_one,
    mlp_moment_two,
    vectors,
    vector_moment_one,
    vector_moment_two,
):
    f32 = jnp.float32
    bf16 = jnp.bfloat16
    contract_rows = (((0,), (0,)), ((), ()))
    contract_cols = (((1,), (1,)), ((), ()))
    tok_rows = inputs.shape[1]
    length = tok_rows * lax.axis_size("seq")
    group_size = H // KV
    score_scale = HD ** (-0.5)
    attn_w, vec_w = (
        lax.all_gather(attn_weight.astype(bf16), "fsdp", axis=0, tiled=True),
        lax.all_gather(vectors.astype(bf16), "fsdp", axis=0, tiled=True),
    )
    mlp_w = lax.all_gather(mlp_weight.astype(bf16), "fsdp", axis=0, tiled=True)
    gain_all = vec_w.astype(f32)
    gain_one = gain_all[:D]
    gain_two = gain_all[D : 2 * D]
    biases = gain_all[2 * D :]
    x_rows = inputs[0].astype(f32)
    inv_one = lax.rsqrt(jnp.mean(x_rows * x_rows, axis=-1, keepdims=True) + norm_eps)
    unit_one = x_rows * inv_one
    normed = (unit_one * gain_one).astype(bf16)
    projected = jnp.dot(normed, attn_w[:, :QKV], preferred_element_type=f32) + biases
    cos_local, sin_local = rotary_tables(lax.axis_index("seq") * tok_rows, tok_rows)
    query_rows = rotate(projected[:, :D].reshape(tok_rows, H, HD), cos_local, sin_local).astype(
        bf16
    )
    key_rows = rotate(
        projected[:, D : D + KV * HD].reshape(tok_rows, KV, HD), cos_local, sin_local
    ).astype(bf16)
    value_rows = projected[:, D + KV * HD :].reshape(tok_rows, KV, HD).astype(bf16)
    query_heads, key_heads, value_heads = (
        lax.all_to_all(query_rows, "seq", split_axis=1, concat_axis=0, tiled=True),
        lax.all_to_all(key_rows, "seq", split_axis=1, concat_axis=0, tiled=True),
        lax.all_to_all(value_rows, "seq", split_axis=1, concat_axis=0, tiled=True),
    )
    kv_local = key_heads.shape[1]
    grouped_q = query_heads.reshape(length, kv_local, group_size, HD)
    causal = jnp.arange(length)[:, None] >= jnp.arange(length)[None, :]

    def score_block(queries_in, keys_in):
        raw_scores = (
            jnp.einsum("lkgd,mkd->kglm", queries_in, keys_in, preferred_element_type=f32)
            * score_scale
        )
        return jnp.where(causal, raw_scores, -1e30)

    scores = score_block(grouped_q, key_heads)
    row_max = jnp.max(scores, axis=-1, keepdims=True)
    log_total = row_max + jnp.log(jnp.sum(jnp.exp(scores - row_max), axis=-1, keepdims=True))
    attn_probs = jnp.exp(scores - log_total).astype(bf16)
    attended_heads = jnp.einsum(
        "kglm,mkd->lkgd", attn_probs, value_heads, preferred_element_type=f32
    )
    attended_heads = attended_heads.astype(bf16).reshape(length, kv_local * group_size, HD)
    attended = lax.all_to_all(
        attended_heads, "seq", split_axis=0, concat_axis=1, tiled=True
    ).reshape(tok_rows, D)
    branch = jnp.dot(attended, attn_w[:, QKV:], preferred_element_type=f32)
    middle = x_rows + branch
    inv_two = lax.rsqrt(jnp.mean(middle * middle, axis=-1, keepdims=True) + norm_eps)
    unit_two = middle * inv_two
    second = (unit_two * gain_two).astype(bf16)
    gate_up = jnp.dot(second, mlp_w[:, : 2 * FF], preferred_element_type=f32)
    gate_value = gate_up[:, :FF]
    up_value = gate_up[:, FF:]
    sigmoid_gate = jax.nn.sigmoid(gate_value)
    act_value = gate_value * sigmoid_gate
    hidden = (act_value * up_value).astype(bf16)
    down_out = lax.dot_general(
        hidden, mlp_w[:, 2 * FF :], contract_cols, preferred_element_type=f32
    )
    output = (middle + down_out).astype(bf16)[None]
    mlp_w = lax.all_gather(mlp_weight.astype(bf16), "fsdp", axis=0, tiled=True)
    back_rows = cotangent[0]
    d_hidden = jnp.dot(back_rows, mlp_w[:, 2 * FF :], preferred_element_type=f32)
    d_gate = d_hidden * up_value * (sigmoid_gate * (1.0 + gate_value * (1.0 - sigmoid_gate)))
    d_up = d_hidden * act_value
    d_gate_up = jnp.concatenate([d_gate, d_up], axis=1).astype(bf16)
    d_second = lax.dot_general(
        d_gate_up, mlp_w[:, : 2 * FF], contract_cols, preferred_element_type=f32
    )
    gate_part = lax.dot_general(second, d_gate_up, contract_rows, preferred_element_type=f32)
    down_part = lax.dot_general(back_rows, hidden, contract_rows, preferred_element_type=f32)
    mlp_part = lax.psum_scatter(
        jnp.concatenate([gate_part, down_part], axis=1), "fsdp", scatter_dimension=0, tiled=True
    )
    scaled_two = d_second * gain_two
    d_gain_two = jnp.sum(d_second * unit_two, axis=0)
    d_middle = back_rows.astype(f32) + inv_two * (
        scaled_two - unit_two * jnp.mean(scaled_two * unit_two, axis=-1, keepdims=True)
    )
    attn_w = lax.all_gather(attn_weight.astype(bf16), "fsdp", axis=0, tiled=True)
    d_branch = d_middle.astype(bf16)
    d_attended = lax.dot_general(
        d_branch, attn_w[:, QKV:], contract_cols, preferred_element_type=f32
    )
    d_attended = d_attended.astype(bf16).reshape(tok_rows, H, HD)
    d_att_heads = lax.all_to_all(d_attended, "seq", split_axis=1, concat_axis=0, tiled=True)
    d_grouped = d_att_heads.reshape(length, kv_local, group_size, HD)
    scores = score_block(grouped_q, key_heads)
    probs_full = jnp.exp(scores - log_total)
    probs_low = probs_full.astype(bf16)
    d_probs = jnp.einsum("lkgd,mkd->kglm", d_grouped, value_heads, preferred_element_type=f32)
    row_dot = jnp.sum(probs_full * d_probs, axis=-1, keepdims=True)
    d_scores = (probs_full * (d_probs - row_dot)).astype(bf16)
    d_query = (
        jnp.einsum("kglm,mkd->lkgd", d_scores, key_heads, preferred_element_type=f32) * score_scale
    )
    d_keys = (
        jnp.einsum("kglm,lkgd->mkd", d_scores, grouped_q, preferred_element_type=f32) * score_scale
    )
    d_values = jnp.einsum("kglm,lkgd->mkd", probs_low, d_grouped, preferred_element_type=f32)
    cos_whole, sin_whole = rotary_tables(0, length)
    d_query = unrotate(
        d_query.reshape(length, kv_local * group_size, HD), cos_whole, sin_whole
    ).astype(bf16)
    d_keys = unrotate(d_keys, cos_whole, sin_whole).astype(bf16)
    d_values = d_values.astype(bf16)
    dq_rows, dk_rows, dv_rows = (
        lax.all_to_all(d_query, "seq", split_axis=0, concat_axis=1, tiled=True),
        lax.all_to_all(d_keys, "seq", split_axis=0, concat_axis=1, tiled=True),
        lax.all_to_all(d_values, "seq", split_axis=0, concat_axis=1, tiled=True),
    )
    d_projected = jnp.concatenate(
        [
            dq_rows.reshape(tok_rows, D),
            dk_rows.reshape(tok_rows, KV * HD),
            dv_rows.reshape(tok_rows, KV * HD),
        ],
        axis=1,
    )
    d_normed = lax.dot_general(
        d_projected, attn_w[:, :QKV], contract_cols, preferred_element_type=f32
    )
    d_biases = jnp.sum(d_projected.astype(f32), axis=0)
    scaled_one = d_normed * gain_one
    d_gain_one = jnp.sum(d_normed * unit_one, axis=0)
    input_grad = d_middle + inv_one * (
        scaled_one - unit_one * jnp.mean(scaled_one * unit_one, axis=-1, keepdims=True)
    )
    attn_term = jnp.concatenate(
        [
            lax.dot_general(normed, d_projected, contract_rows, preferred_element_type=f32),
            lax.dot_general(attended, d_branch, contract_rows, preferred_element_type=f32),
        ],
        axis=1,
    )
    vec_term = jnp.concatenate([d_gain_one, d_gain_two, d_biases])
    attn_part, vec_part = (
        lax.psum_scatter(attn_term, "fsdp", scatter_dimension=0, tiled=True),
        lax.psum_scatter(vec_term, "fsdp", scatter_dimension=0, tiled=True),
    )
    attn_grad, mlp_grad, vec_grad = (
        lax.psum(attn_part.astype(jnp.bfloat16), "seq").astype(jnp.float32),
        lax.psum(mlp_part.astype(jnp.bfloat16), "seq").astype(jnp.float32),
        lax.psum(vec_part.astype(jnp.bfloat16), "seq").astype(jnp.float32),
    )
    attn_one, attn_two, attn_new = adam_update(
        attn_weight, attn_moment_one, attn_moment_two, attn_grad, 0.05
    )
    mlp_one, mlp_two, mlp_new = adam_update(
        mlp_weight, mlp_moment_one, mlp_moment_two, mlp_grad, 0.02
    )
    vec_one, vec_two, vec_new = adam_update(
        vectors, vector_moment_one, vector_moment_two, vec_grad, 0.5
    )
    return (
        output,
        input_grad[None],
        attn_one,
        attn_two,
        attn_new,
        mlp_one,
        mlp_two,
        mlp_new,
        vec_one,
        vec_two,
        vec_new,
    )


def solution(mesh):
    return jax.shard_map(
        shards,
        mesh=mesh,
        in_specs=(
            P("fsdp", "seq", None),
            P("fsdp", "seq", None),
            P("fsdp", None),
            P("fsdp", None),
            P("fsdp", None),
            P("fsdp", None),
            P("fsdp", None),
            P("fsdp", None),
            P("fsdp"),
            P("fsdp"),
            P("fsdp"),
        ),
        out_specs=(
            P("fsdp", "seq", None),
            P("fsdp", "seq", None),
            P("fsdp", None),
            P("fsdp", None),
            P("fsdp", None),
            P("fsdp", None),
            P("fsdp", None),
            P("fsdp", None),
            P("fsdp"),
            P("fsdp"),
            P("fsdp"),
        ),
        check_vma=False,
    )
```

profile of v0, /device:TPU:1, one launch (start us, length us, event | category | flops | bytes accessed | tf_op | source)
XLA Modules:
  0.0 2091.0 jit_solution(2191071771181044671)
XLA Ops:
  7.2 1.7 convert_element_type.129
  9.0 3.0 convert_element_type.139
  13.5 329.5 %all-reduce = bf16[5120]{0:T(1024)(128)(2,1)S(1)} all-reduce(bf16[5120]{0:T(1024)(128)(2,1)S(1)} %dynamic-update-slice), channel_id=1, replica_groups=mesh['seq'=2,'fsdp'=64] {'fsdp'}, use_global_device_ids=true, to_apply=%add | all-reduce | flops 5120 | bytes 20480
  343.8 3.8 fusion.26
  349.9 3.5 all-to-all-start.2
  354.4 1.6 fusion.75
  356.1 6.6 all-to-all-done.2
  362.7 3.3 all-to-all-start.1
  366.0 1.5 copy_bitcast_fusion.1
  367.8 2.6 all-to-all-done.1
  370.4 3.3 all-to-all-start
  374.3 2.7 all-to-all-done
  378.6 4.0 all-to-all-start.3
  383.2 5.6 all-to-all-done.3
  389.1 3.7 multiply_reduce_fusion.2
  393.3 39.2 %all-gather.5.cloned.1.call-done = bf16[1536,26880]{1,0:T(8,128)(2,1)} async-done(((bf16[24,26880]{1,0:T(8,128)(2,1)}), bf16[1536,26880]{1,0:T(8,128)(2,1)}) %all-gather.5.cloned.1.call-update) | async-done | bytes 82575376 | tf_op jit(solution)/shard_map/all_gather | solution.py:75
  432.5 23.6 %fusion.2 = f32[128,17920]{1,0:T(8,128)} fusion(bf16[1536,26880]{1,0:T(8,128)(2,1)} %all-gather.5.cloned.1.call-done, f32[128,1536]{1,0:T(8,128)S(1)} %get-tuple-element.50, f32[1536]{0:T(1024)S(1)} %get-tuple-element.41, f32[128]{0:T(128)} %add_rsqrt_fusion), kind=kOutput, calls=%fused_computation.3 | convolution fusion | flops 7047020544 | bytes 65018368 | tf_op jit(solution)/shard_map/dot_general | solution.py:125
  456.1 17.3 multiply_convert_fusion.1
  473.4 26.2 %multiply_reduce_fusion = (f32[1536]{0:T(1024)}, f32[128]{0:T(128)}, f32[128,1536]{1,0:T(8,128)}) fusion(f32[128,1536]{1,0:T(8,128)S(1)} %get-tuple-element.50, f32[128]{0:T(128)} %add_rsqrt_fusion, f32[1536]{0:T(1024)S(1)} %get-tuple-element.41, bf16[1536,26880]{1,0:T(8,128)(2,1)} %all-gather.5.cloned.1.call-done, ...), kind=kOutput, calls=%fused_computation.78 | convolution fusion | flops 7056783872 | bytes 61223936 | tf_op jit(solution)/shard_map/dot_general | solution.py:141
  500.2 1.6 multiply_add_fusion
  501.9 4.3 fusion.29
  507.0 3.5 all-to-all-start.4
  510.5 1.4 broadcast_multiply_fusion.1
  513.1 3.9 all-to-all-done.4
  520.0 2.9 fusion.38
  523.4 1.5 reduce.3
  525.7 4.1 all-to-all-start.7
  529.8 1.7 fusion.61
  534.6 3.9 all-to-all-start.6
  541.6 3.5 all-to-all-start.5
  545.2 5.1 fusion.71
  552.9 1.9 fusion.84
  555.2 1.3 slice-done.2
  556.5 7.8 pad_maximum_fusion.1
  565.2 25.8 %convolution_bitcast_fusion = f32[1536,8960]{1,0:T(8,128)} fusion(bf16[128,8960]{1,0:T(8,128)(2,1)} %get-tuple-element.28, bf16[1,128,1536]{2,1,0:T(8,128)(2,1)S(1)} %copy-done.13), kind=kOutput, calls=%fused_computation.5 | convolution fusion | flops 3523215360 | bytes 57737216 | tf_op jit(solution)/shard_map/dot_general | solution.py:145
  591.1 46.1 %fusion.17 = f32[1536,17920]{1,0:T(8,128)} fusion(bf16[128,8960]{1,0:T(8,128)(2,1)} %get-tuple-element.27, bf16[128,8960]{1,0:T(8,128)(2,1)} %get-tuple-element.26, f32[128,1536]{1,0:T(8,128)S(1)} %copy-done.8, f32[1536]{0:T(1024)S(1)} %get-tuple-element.41, f32[128]{0:T(128)S(1)} %copy-done.29), kind=kOutput, calls=%fused_computation.27 | convolution fusion | flops 7056195584 | bytes 115481088 | tf_op jit(solution)/shard_map/dot_general | solution.py:144
  637.1 110.5 %pad_maximum_fusion = f32[1536,26880]{1,0:T(8,128)} fusion(f32[1536,8960]{1,0:T(8,128)} %convolution_bitcast_fusion, f32[1536,17920]{1,0:T(8,128)} %fusion.17), kind=kLoop, calls=%fused_computation | loop fusion | flops 41287680 | bytes 330301440 | tf_op jit(solution)/shard_map/concatenate | solution.py:147
  748.4 15.4 fusion.35
  764.0 23.6 %reduce-scatter.3.cloned.1.call-done = f32[24,3584]{1,0:T(8,128)} async-done(((f32[1536,3584]{1,0:T(8,128)}), f32[24,3584]{1,0:T(8,128)}) %reduce-scatter.3.cloned.1.call-update) | async-done | bytes 344080 | tf_op jit(solution)/shard_map/reduce_scatter | solution.py:212
  787.6 1.7 convert_element_type.152
  789.3 948.3 %reduce-scatter.5.cloned.1.call-done = f32[24,26880]{1,0:T(8,128)} async-done(((f32[1536,26880]{1,0:T(8,128)}), f32[24,26880]{1,0:T(8,128)}) %reduce-scatter.5.cloned.1.call-update) | async-done | bytes 2580496 | tf_op jit(solution)/shard_map/reduce_scatter | solution.py:146
  1737.6 2.9 convert_element_type.154
  1740.6 6.0 fusion.58
  1746.6 321.1 %all-reduce.1 = bf16[5120]{0:T(1024)(128)(2,1)S(1)} all-reduce(f32[5120]{0:T(1024)S(1)} %pad_maximum_fusion.9), channel_id=4, replica_groups=mesh['seq'=2,'fsdp'=64] {'fsdp'}, use_global_device_ids=true, to_apply=%region_14.15.clone | all-reduce | flops 5120 | bytes 30720
  2067.7 4.0 psum.23
  2072.3 2.4 fusion.57
  2074.7 2.5 multiply_subtract_fusion.1
  2077.2 7.0 multiply_subtract_fusion
  (161 shorter events, 26.7 us)
Async XLA Ops:
  7.2 336.7 %all-gather.3.cloned.1.call-start = ((), (), s32[]{:S(2)}) async-start(), calls=%async_computation.10 | async-start | bytes 11182080 | tf_op jit(solution)/shard_map/all_gather | solution.py:72
  8.9 3.1 copy-start.36
  8.9 3.1 copy-start.35
  8.9 334.6 %copy-start.3 = (bf16[1,128,1536]{2,1,0:T(8,128)(2,1)S(1)}, bf16[1,128,1536]{2,1,0:T(8,128)(2,1)}, u32[]{:S(2)}) copy-start(bf16[1,128,1536]{2,1,0:T(8,128)(2,1)} %param.11) | copy-start | bytes 1179652
  9.0 423.6 %all-gather.5.cloned.1.call-start = ((), (), s32[]{:S(2)}) async-start(), calls=%async_computation.11 | async-start | bytes 83865600 | tf_op jit(solution)/shard_map/all_gather | solution.py:75
  343.8 3.9 copy-start.31
  343.8 3.9 copy-start.26
  349.9 12.8 all-to-all-start.2
  362.7 7.7 all-to-all-start.1
  370.4 7.1 copy-start.21
  370.4 6.7 all-to-all-start
  378.6 10.2 all-to-all-start.3
  389.1 3.7 copy-start.9
  392.8 80.7 %copy-start.7 = (f32[128,1536]{1,0:T(8,128)}, f32[128,1536]{1,0:T(8,128)S(1)}, u32[]{:S(2)}) copy-start(f32[128,1536]{1,0:T(8,128)S(1)} %get-tuple-element.50) | copy-start | bytes 2359300
  432.5 23.6 %copy-start.12 = (bf16[1,128,1536]{2,1,0:T(8,128)(2,1)S(1)}, bf16[1,128,1536]{2,1,0:T(8,128)(2,1)}, u32[]{:S(2)}) copy-start(bf16[1,128,1536]{2,1,0:T(8,128)(2,1)} %param.12) | copy-start | bytes 1179652
  501.9 43.3 %copy-start.1 = (f32[128,1536]{1,0:T(8,128)}, f32[128,1536]{1,0:T(8,128)S(1)}, u32[]{:S(2)}) copy-start(f32[128,1536]{1,0:T(8,128)S(1)} %multiply_add_fusion) | copy-start | bytes 2359300
  507.0 9.9 all-to-all-start.4
  522.9 8.6 copy-start.23
  525.7 8.9 all-to-all-start.7
  529.8 2.5 copy-start.22
  529.8 2.5 copy-start.25
  532.7 12.5 copy-start.10
  534.6 7.0 all-to-all-start.6
  541.6 10.9 all-to-all-start.5
  545.1 7.8 copy-start.27
  545.1 7.8 copy-start.32
  545.1 242.5 %reduce-scatter.3.cloned.1.call-start = ((), (), s32[]{:S(2)}) async-start(), calls=%async_computation.12 | async-start | bytes 22364160 | tf_op jit(solution)/shard_map/reduce_scatter | solution.py:212
  551.3 3.5 copy-start.17
  551.3 3.5 slice-start
  552.5 2.3 copy-start.19
  552.9 3.6 slice-start.2
  564.2 1173.3 %reduce-scatter.5.cloned.1.call-start = ((), (), s32[]{:S(2)}) async-start(), calls=%async_computation.13 | async-start | bytes 167731200 | tf_op jit(solution)/shard_map/reduce_scatter | solution.py:146
  565.2 25.8 %copy-start.8 = (f32[128,1536]{1,0:T(8,128)S(1)}, f32[128,1536]{1,0:T(8,128)}, u32[]{:S(2)}) copy-start(f32[128,1536]{1,0:T(8,128)} %copy-done.7) | copy-start | bytes 2359300
  565.2 25.8 %copy-start.29 = (f32[128]{0:T(128)S(1)}, f32[128]{0:T(128)}, u32[]{:S(2)}) copy-start(f32[128]{0:T(128)} %add_rsqrt_fusion) | copy-start | bytes 1540
  747.7 1327.0 %all-reduce.5.cloned.1.call-start = ((), (), s32[]{:S(2)}) async-start(), calls=%async_computation.14 | async-start | bytes 2924544 | tf_op jit(solution)/shard_map/psum | solution.py:216
  748.4 15.4 copy-start.6
  748.4 15.4 copy-start.18
  748.4 15.4 copy-start.20
  789.3 951.2 %copy-start.4 = (bf16[1,128,1536]{2,1,0:T(8,128)(2,1)S(1)}, bf16[1,128,1536]{2,1,0:T(8,128)(2,1)}, u32[]{:S(2)}) copy-start(bf16[1,128,1536]{2,1,0:T(8,128)(2,1)} %param.11) | copy-start | bytes 1179652
  789.3 951.2 %copy-start.28 = (f32[1536]{0:T(1024)S(1)}, f32[1536]{0:T(1024)}, u32[]{:S(2)}) copy-start(f32[1536]{0:T(1024)} %copy-done.26) | copy-start | bytes 18436
  789.3 951.2 %copy-start.33 = (f32[128]{0:T(128)S(1)}, f32[128]{0:T(128)}, u32[]{:S(2)}) copy-start(f32[128]{0:T(128)} %copy-done.31) | copy-start | bytes 1540
  1740.5 6.0 copy-start.30
  1740.5 331.2 %copy-start.37 = (f32[80]{0:T(128)S(1)}, f32[80]{0:T(128)}, u32[]{:S(2)}) copy-start(f32[80]{0:T(128)} %param.19) | copy-start | bytes 964
  1740.5 331.2 %copy-start.38 = (f32[80]{0:T(128)S(1)}, f32[80]{0:T(128)}, u32[]{:S(2)}) copy-start(f32[80]{0:T(128)} %param.21) | copy-start | bytes 964
  1740.6 331.2 %copy-start.39 = (f32[80]{0:T(128)S(1)}, f32[80]{0:T(128)}, u32[]{:S(2)}) copy-start(f32[80]{0:T(128)} %param.20) | copy-start | bytes 964
  1740.6 331.7 %copy-start.2 = (f32[128,1536]{1,0:T(8,128)S(1)}, f32[128,1536]{1,0:T(8,128)}, u32[]{:S(2)}) copy-start(f32[128,1536]{1,0:T(8,128)} %copy-done.1) | copy-start | bytes 2359300
  1746.5 330.7 %copy-start = (f32[24,26880]{1,0:T(8,128)S(1)}, f32[24,26880]{1,0:T(8,128)}, u32[]{:S(2)}) copy-start(f32[24,26880]{1,0:T(8,128)} %param.16) | copy-start | bytes 7741444
  2074.7 2.5 copy-start.14
  (8 other events, 10.4 us)
Sparse Core Ops, SparseCore 0:
  11.9 93.1 all-gather.2
  108.9 323.5 all-gather.4
  564.4 223.2 reduce-scatter.2
  793.9 943.6 reduce-scatter.4
  1740.7 56.4 all-reduce.4
where the time goes:
time: 2100 us; the launch traced here: 2090 us
  waiting for transfers between devices  1030 us (49%)
  blocking collectives  655 us (31%)
  matrix products  185 us (9%)
  other arithmetic  155 us (7%)
  starting transfers between devices  29.4 us (1%)
    reduce_scatter x1, waiting for transfers between devices, shards(): lax.psum_scatter(jnp.concatenate([gate_part, down_part], axis=1), 'fsdp',...  948 us
    unnamed x2, blocking collectives  651 us
    concatenate x1, other arithmetic, shards(): jnp.concatenate([gate_part, down_part], axis=1)  111 us
    dot_general x1, matrix products, shards(): lax.dot_general(second, d_gate_up, contract_rows, preferred_element_type=...  46.1 us
  transfers between devices with their start and end apart: 13, of which 9 were waited for; matrix products, arithmetic and copies ran while one was open for 12% of the time, Pallas kernels for 0%

commit v1 on v0

v1 whole, which is shorter than its diff:
```python
import jax
import jax.numpy as jnp
from jax import lax
from jax.experimental import pallas as pl
from jax.experimental.pallas import tpu as pltpu
from jax.sharding import Mesh
from jax.sharding import PartitionSpec as P

D = 1536
H = 12
KV = 2
HD = 128
FF = 8960
STEP = 10
QKV = 2048
ROWS = 24
TOK = 128
LEN = 256
HALF = D // 2
GROUP = H // KV
COLS = GROUP * HD + 2 * HD
FFT = 1152

norm_eps = 1e-06
rope_base = 1000000.0
f32 = jnp.float32
bf16 = jnp.bfloat16
contract_rows = (((0,), (0,)), ((), ()))
contract_cols = (((1,), (1,)), ((), ()))
score_scale = HD ** (-0.5)
FSDP = ("z", "yh", "x", "core")


def dot(a, b):
    return jnp.dot(a, b, preferred_element_type=f32)


def dot_tn(a, b):
    return lax.dot_general(a, b, contract_rows, preferred_element_type=f32)


def dot_nt(a, b):
    return lax.dot_general(a, b, contract_cols, preferred_element_type=f32)


def split_dot(a, b):
    high = a.astype(bf16)
    low = (a - high.astype(f32)).astype(bf16)
    return dot(high, b) + dot(low, b)


def ring_send(values, axis, shift):
    size = {"z": 4, "x": 4, "yh": 2, "core": 2, "seq": 2}[axis]
    return lax.ppermute(values, axis, [(i, (i + shift) % size) for i in range(size)])


def y_send(values, shift):
    place = lambda y: (y % 2) * 2 + y // 2
    return lax.ppermute(
        values, ("seq", "yh"), [(place(i), place((i + shift) % 4)) for i in range(4)]
    )


def swap_both(values):
    return lax.ppermute(values, ("yh", "core"), [(i, 3 - i) for i in range(4)])


def ring_gather(values, send):
    return jnp.concatenate([values, send(values, 1), send(values, -1), send(values, 2)], axis=0)


def ring_reduce(values, send):
    rows = values.shape[0] // 4
    parts = [values[i * rows : (i + 1) * rows] for i in range(4)]
    low = [p.astype(bf16) for p in parts]
    got = [send(low[1], -1), send(low[2], 1), send(low[3], 2)]
    return parts[0] + got[0].astype(f32) + got[1].astype(f32) + got[2].astype(f32)


def pair_reduce(values, send):
    rows = values.shape[0] // 2
    return values[:rows] + send(values[rows:].astype(bf16)).astype(f32)


def gather_rows(values):
    values = ring_gather(values, lambda v, k: ring_send(v, "x", k))
    values = jnp.concatenate([values, ring_send(values, "yh", 1)], axis=0)
    values = ring_gather(values, lambda v, k: ring_send(v, "z", k))
    return jnp.concatenate([values, ring_send(values, "core", 1)], axis=0)


def reduce_rows(values):
    values = pair_reduce(values, lambda v: ring_send(v, "core", 1))
    values = ring_reduce(values, lambda v, k: ring_send(v, "z", k))
    values = pair_reduce(values, lambda v: ring_send(v, "yh", 1))
    return ring_reduce(values, lambda v, k: ring_send(v, "x", k))


def gather_tokens(values):
    values = ring_gather(values, y_send)
    return jnp.concatenate([values, ring_send(values, "core", 1)], axis=0)


def reduce_tokens(values):
    values = pair_reduce(values, lambda v: ring_send(v, "core", 1))
    return ring_reduce(values, y_send)


def near(index):
    return jnp.where(index == 1, -1, jnp.where(index == 0, 0, index - 1))


def gathered_rows(shape, dim):
    j = lax.broadcasted_iota(jnp.int32, shape, dim)
    r, xi, yi, zi, ci = j % 24, (j // 24) % 4, (j // 96) % 2, (j // 192) % 4, j // 768
    z = (lax.axis_index("z") + near(zi) + 4) % 4
    x = (lax.axis_index("x") + near(xi) + 4) % 4
    yh = (lax.axis_index("yh") + yi) % 2
    core = (lax.axis_index("core") + ci) % 2
    return z * 384 + yh * 192 + x * 48 + core * 24 + r


def mlp_rows(shape, dim):
    j = lax.broadcasted_iota(jnp.int32, shape, dim)
    r, core, yh, x, z = j % 24, (j // 24) % 2, (j // 48) % 2, (j // 96) % 4, j // 384
    return z * 384 + yh * 192 + x * 48 + core * 24 + r


def rotary_tables(positions):
    half_dim = HD // 2
    freqs = rope_base ** (-jnp.arange(half_dim, dtype=f32) * 2.0 / HD)
    angles = positions.astype(f32)[:, None] * freqs[None, :]
    cos, sin = jnp.cos(angles), jnp.sin(angles)
    return jnp.concatenate([cos, cos], axis=1), jnp.concatenate([-sin, sin], axis=1)


def causal_mask(half):
    row = (lax.broadcasted_iota(jnp.int32, (LEN, LEN), 0) + half * TOK) % LEN
    col = (lax.broadcasted_iota(jnp.int32, (LEN, LEN), 1) + half * TOK) % LEN
    return row >= col


def attend_kernel(half_ref, qkv_ref, bias_ref, cos_ref, sin_ref, low_ref, out_ref, log_ref):
    cos, sin = cos_ref[...], sin_ref[...]
    mask = causal_mask(half_ref[0])

    def rotated(start):
        z = qkv_ref[:, start : start + HD] + bias_ref[:, start : start + HD]
        return (z * cos + pltpu.roll(z, HD // 2, 1) * sin).astype(bf16)

    key = rotated(GROUP * HD)
    low_ref[:, GROUP * HD : (GROUP + 1) * HD] = key
    value = (qkv_ref[:, (GROUP + 1) * HD :] + bias_ref[:, (GROUP + 1) * HD :]).astype(bf16)
    low_ref[:, (GROUP + 1) * HD :] = value
    for h in range(GROUP):
        query = rotated(h * HD)
        low_ref[:, h * HD : (h + 1) * HD] = query
        scores = jnp.where(mask, dot_nt(query, key) * score_scale, -1e30)
        top = jnp.max(scores, axis=-1, keepdims=True)
        total = top + jnp.log(jnp.sum(jnp.exp(scores - top), axis=-1, keepdims=True))
        log_ref[h] = jnp.broadcast_to(total, (LEN, HD))
        probs = jnp.exp(scores - total).astype(bf16)
        out_ref[:, h * HD : (h + 1) * HD] = dot(probs, value).astype(bf16)


def attend(half, qkv, bias, cos, sin):
    vmem = pl.BlockSpec(memory_space=pltpu.VMEM)
    return pl.pallas_call(
        attend_kernel,
        out_shape=(
            jax.ShapeDtypeStruct((LEN, COLS), bf16),
            jax.ShapeDtypeStruct((LEN, GROUP * HD), bf16),
            jax.ShapeDtypeStruct((GROUP, LEN, HD), f32),
        ),
        in_specs=[pl.BlockSpec(memory_space=pltpu.SMEM)] + [vmem] * 4,
        out_specs=(vmem, vmem, vmem),
        compiler_params=pltpu.CompilerParams(vmem_limit_bytes=32 * 1024 * 1024),
    )(half, qkv, bias, cos, sin)


def attend_back_kernel(half_ref, low_ref, grad_ref, log_ref, cos_ref, sin_ref, out_ref, sum_ref):
    cos, sin = cos_ref[...], sin_ref[...]
    mask = causal_mask(half_ref[0])
    key = low_ref[:, GROUP * HD : (GROUP + 1) * HD]
    value = low_ref[:, (GROUP + 1) * HD :]

    def unrotated(z):
        return (z * cos - pltpu.roll(z, HD // 2, 1) * sin).astype(bf16)

    def put(start, block):
        out_ref[:, start : start + HD] = block
        sum_ref[:, start : start + HD] = jnp.sum(block.astype(f32), axis=0, keepdims=True)

    d_key = jnp.zeros((LEN, HD), f32)
    d_value = jnp.zeros((LEN, HD), f32)
    for h in range(GROUP):
        query = low_ref[:, h * HD : (h + 1) * HD]
        grad = grad_ref[:, h * HD : (h + 1) * HD]
        scores = jnp.where(mask, dot_nt(query, key) * score_scale, -1e30)
        total = log_ref[h]
        probs = jnp.exp(scores - jnp.concatenate([total, total], axis=1))
        d_probs = dot_nt(grad, value)
        delta = jnp.sum(probs * d_probs, axis=-1, keepdims=True)
        d_scores = (probs * (d_probs - delta)).astype(bf16)
        put(h * HD, unrotated(dot(d_scores, key) * score_scale))
        d_key += dot_tn(d_scores, query)
        d_value += dot_tn(probs.astype(bf16), grad)
    put(GROUP * HD, unrotated(d_key * score_scale))
    put((GROUP + 1) * HD, d_value.astype(bf16))


def attend_back(half, low, grad, logs, cos, sin):
    vmem = pl.BlockSpec(memory_space=pltpu.VMEM)
    return pl.pallas_call(
        attend_back_kernel,
        out_shape=(
            jax.ShapeDtypeStruct((LEN, COLS), bf16),
            jax.ShapeDtypeStruct((1, COLS), f32),
        ),
        in_specs=[pl.BlockSpec(memory_space=pltpu.SMEM)] + [vmem] * 5,
        out_specs=(vmem, vmem),
        compiler_params=pltpu.CompilerParams(vmem_limit_bytes=32 * 1024 * 1024),
    )(half, low, grad, logs, cos, sin)


def adam_update(weight, moment_one, moment_two, gradient, step_rate):
    moment_one = 0.9 * moment_one + 0.1 * gradient
    moment_two = 0.95 * moment_two + 0.05 * gradient * gradient
    first_hat = moment_one / (1.0 - 0.9**STEP)
    second_hat = moment_two / (1.0 - 0.95**STEP)
    updated = weight - step_rate * (first_hat / (jnp.sqrt(second_hat) + 1e-08) + 0.1 * weight)
    return (moment_one, moment_two, updated)


def one_hot(rows_of, shift=0):
    row = lax.broadcasted_iota(jnp.int32, (D, D), 0)
    return (row == (rows_of((D, D), 1) + shift) % D).astype(bf16)


def shards(
    inputs,
    cotangent,
    attn_weight,
    attn_moment_one,
    attn_moment_two,
    mlp_weight,
    mlp_moment_one,
    mlp_moment_two,
    vectors,
    vector_moment_one,
    vector_moment_two,
):
    half = lax.axis_index("seq")
    me = lax.axis_index("yh") * 2 + lax.axis_index("core")
    halves = half.astype(jnp.int32).reshape(1)
    x_own, dy_own = inputs[0], cotangent[0]
    x_all = jnp.concatenate([x_own, ring_send(x_own, "seq", 1)], axis=0)

    to_rel = one_hot(gathered_rows)
    to_feat = one_hot(gathered_rows, half * HALF)
    to_mlp = one_hot(mlp_rows)

    attn_low = attn_weight.astype(bf16)
    own_cols = lambda a, start, width: lax.dynamic_slice_in_dim(a, start + half * width, width, 1)
    vec_block = jnp.pad(vectors.astype(bf16)[None, :], ((0, ROWS - 1), (0, 48)))
    proj_block = jnp.concatenate(
        [
            own_cols(attn_low, 0, GROUP * HD),
            own_cols(attn_low, D, HD),
            own_cols(attn_low, D + KV * HD, HD),
            vec_block,
        ],
        axis=1,
    )
    out_block = dot(attn_low[:, QKV:], to_mlp).astype(bf16)
    proj_all = gather_rows(proj_block)
    out_w = gather_rows(out_block)
    proj_w = proj_all[:, :COLS]

    mlp_low = jnp.pad(
        mlp_weight.astype(bf16).reshape(ROWS, 3, FF), ((0, 0), (0, 0), (0, 8 * FFT - FF))
    )
    mlp_half = lax.dynamic_slice_in_dim(mlp_low, half * 4 * FFT, 4 * FFT, 2)
    mlp_blocks = mlp_half.reshape(ROWS, 3, 4, FFT).transpose(2, 0, 1, 3).reshape(4, ROWS, 3 * FFT)
    block = lambda a, i: lax.dynamic_index_in_dim(a, i, 0, keepdims=False)
    mlp_rel = jnp.stack(
        [
            block(mlp_blocks, me),
            ring_send(block(mlp_blocks, me ^ 1), "core", 1),
            ring_send(block(mlp_blocks, me ^ 2), "yh", 1),
            swap_both(block(mlp_blocks, me ^ 3)),
        ]
    )
    mlp_rows_own = jnp.concatenate([block(mlp_rel, me ^ q) for q in range(4)], axis=0)
    mlp_w = lax.all_gather(mlp_rows_own, ("z", "x"), axis=0, tiled=True)

    block_row = lax.broadcasted_iota(jnp.int32, (64, D), 0) * ROWS
    pick = (block_row == gathered_rows((64, D), 1)).astype(bf16)
    vec_all = dot(pick, proj_all[:, COLS:])[:, :80].reshape(1, 5120)
    gain_one = dot(vec_all[:, :D].astype(bf16), to_rel)
    gain_two = dot(vec_all[:, D : 2 * D].astype(bf16), to_mlp)
    bias_all = vec_all[:, 2 * D :]
    bias = jnp.concatenate(
        [
            own_cols(bias_all, 0, GROUP * HD),
            own_cols(bias_all, D, HD),
            own_cols(bias_all, D + KV * HD, HD),
        ],
        axis=1,
    )

    x_rel = dot(x_all, to_rel)
    x_mlp = dot(x_own, to_mlp)
    dy_low = dot(dy_own, to_mlp).astype(bf16)
    dy_all = gather_tokens(dy_low)
    inv_one = lax.rsqrt(jnp.mean(x_rel * x_rel, axis=-1, keepdims=True) + norm_eps)
    unit_one = x_rel * inv_one
    normed = (unit_one * gain_one).astype(bf16)
    cos, sin = rotary_tables((jnp.arange(LEN) + half * TOK) % LEN)
    low, heads_out, logs = attend(halves, dot(normed, proj_w), bias, cos, sin)
    attended = jnp.concatenate(
        [heads_out[:TOK], ring_send(heads_out[TOK:], "seq", 1)], axis=1
    )
    attended_rel = dot(attended, to_feat).astype(bf16)
    middle = x_mlp + dot(attended_rel, out_w)
    inv_two = lax.rsqrt(jnp.mean(middle * middle, axis=-1, keepdims=True) + norm_eps)
    unit_two = middle * inv_two
    second = (unit_two * gain_two).astype(bf16)

    second_all = gather_tokens(second)
    gate_up = dot(second_all, mlp_w[:, : 2 * FFT])
    gate, up = gate_up[:, :FFT], gate_up[:, FFT:]
    sigmoid_gate = jax.nn.sigmoid(gate)
    act = gate * sigmoid_gate
    hidden = (act * up).astype(bf16)
    d_hidden = dot(dy_all, mlp_w[:, 2 * FFT :])
    d_gate = d_hidden * up * (sigmoid_gate * (1.0 + gate * (1.0 - sigmoid_gate)))
    d_gate_up = jnp.concatenate([d_gate, d_hidden * act], axis=1).astype(bf16)
    d_second = reduce_tokens(dot_nt(d_gate_up, mlp_w[:, : 2 * FFT]))
    down = reduce_tokens(dot_nt(hidden, mlp_w[:, 2 * FFT :]))
    output = dot_nt((middle + down).astype(bf16), to_mlp).astype(bf16)[None]
    mlp_term = jnp.concatenate(
        [dot_tn(second_all, d_gate_up).astype(bf16), dot_tn(dy_all, hidden).astype(bf16)], axis=1
    )
    mlp_part = lax.psum_scatter(mlp_term, ("z", "x"), scatter_dimension=0, tiled=True)

    scaled_two = d_second * gain_two
    d_gain_two = jnp.sum(d_second * unit_two, axis=0, keepdims=True)
    d_middle = dy_low.astype(f32) + inv_two * (
        scaled_two - unit_two * jnp.mean(scaled_two * unit_two, axis=-1, keepdims=True)
    )

    d_branch = d_middle.astype(bf16)
    d_attended = dot_nt(dot_nt(d_branch, out_w).astype(bf16), to_feat).astype(bf16)
    d_heads = jnp.concatenate(
        [d_attended[:, :HALF], ring_send(d_attended[:, HALF:], "seq", 1)], axis=0
    )
    d_proj, d_proj_sum = attend_back(halves, low, d_heads, logs, cos, sin)
    d_normed = dot_nt(d_proj, proj_w)
    d_gain_one = jnp.sum(d_normed * unit_one, axis=0, keepdims=True)
    d_normed_own = d_normed[:TOK] + ring_send(d_normed[TOK:].astype(bf16), "seq", 1).astype(f32)
    scaled_one = d_normed_own * gain_one
    unit_own = unit_one[:TOK]
    through_norm = inv_one[:TOK] * (
        scaled_one - unit_own * jnp.mean(scaled_one * unit_own, axis=-1, keepdims=True)
    )
    input_grad = split_dot(d_middle, to_mlp.T) + split_dot(through_norm, to_rel.T)

    bias_zero = jnp.zeros((1, QKV), f32)
    put = lambda a, v, start, width: lax.dynamic_update_slice_in_dim(a, v, start + half * width, 1)
    d_bias = put(bias_zero, d_proj_sum[:, : GROUP * HD], 0, GROUP * HD)
    d_bias = put(d_bias, d_proj_sum[:, GROUP * HD : (GROUP + 1) * HD], D, HD)
    d_bias = put(d_bias, d_proj_sum[:, (GROUP + 1) * HD :], D + KV * HD, HD)
    vec_term = jnp.concatenate(
        [split_dot(d_gain_one, to_rel.T), split_dot(d_gain_two, to_mlp.T), d_bias], axis=1
    )
    vec_term = jnp.pad(vec_term.reshape(64, 80).astype(bf16), ((0, 0), (0, 48)))
    proj_part = reduce_rows(
        jnp.concatenate([dot_tn(normed, d_proj), dot_tn(pick, vec_term)], axis=1)
    )
    out_part = reduce_rows(dot_tn(attended_rel, d_branch))

    proj_low, out_low = proj_part.astype(bf16), out_part.astype(bf16)
    proj_other = ring_send(proj_low, "seq", 1)
    out_grad = out_low.astype(f32) + ring_send(out_low, "seq", 1).astype(f32)
    vec_grad = (proj_low[:1, COLS : COLS + 80].astype(f32) + proj_other[:1, COLS : COLS + 80].astype(f32))[0]
    first = jnp.where(half == 0, proj_low, proj_other).astype(f32)
    last = jnp.where(half == 0, proj_other, proj_low).astype(f32)
    query_end, key_end = GROUP * HD, (GROUP + 1) * HD
    attn_grad = jnp.concatenate(
        [
            first[:, :query_end],
            last[:, :query_end],
            first[:, query_end:key_end],
            last[:, query_end:key_end],
            first[:, key_end:COLS],
            last[:, key_end:COLS],
            split_dot(out_grad, to_mlp.T),
        ],
        axis=1,
    )

    mlp_parts = mlp_part.reshape(4, ROWS, 3 * FFT)
    grad_rel = jnp.stack(
        [
            block(mlp_parts, me),
            ring_send(block(mlp_parts, me ^ 1), "core", 1),
            ring_send(block(mlp_parts, me ^ 2), "yh", 1),
            swap_both(block(mlp_parts, me ^ 3)),
        ]
    )
    grad_half = jnp.stack([block(grad_rel, me ^ q) for q in range(4)])
    grad_other = ring_send(grad_half, "seq", 1)
    grad_all = jnp.concatenate(
        [jnp.where(half == 0, grad_half, grad_other), jnp.where(half == 0, grad_other, grad_half)]
    )
    mlp_grad = (
        grad_all.reshape(8, ROWS, 3, FFT)
        .transpose(1, 2, 0, 3)
        .reshape(ROWS, 3, 8 * FFT)[:, :, :FF]
        .reshape(ROWS, 3 * FF)
        .astype(f32)
    )

    attn_one, attn_two, attn_new = adam_update(
        attn_weight, attn_moment_one, attn_moment_two, attn_grad, 0.05
    )
    mlp_one, mlp_two, mlp_new = adam_update(
        mlp_weight, mlp_moment_one, mlp_moment_two, mlp_grad, 0.02
    )
    vec_one, vec_two, vec_new = adam_update(
        vectors, vector_moment_one, vector_moment_two, vec_grad, 0.5
    )
    return (
        output,
        input_grad[None],
        attn_one,
        attn_two,
        attn_new,
        mlp_one,
        mlp_two,
        mlp_new,
        vec_one,
        vec_two,
        vec_new,
    )


def solution(mesh):
    grid = Mesh(mesh.devices.reshape(2, 4, 2, 4, 2), ("seq",) + FSDP)
    tokens, rows, vector = P(FSDP, "seq", None), P(FSDP, None), P(FSDP)
    return jax.shard_map(
        shards,
        mesh=grid,
        in_specs=(tokens, tokens) + (rows,) * 6 + (vector,) * 3,
        out_specs=(tokens, tokens) + (rows,) * 6 + (vector,) * 3,
        check_vma=False,
    )
```

time: 2100 us -> 539 us (0.26)
  waiting for transfers between devices: 1030 us -> 220 us
  blocking collectives: 655 us -> 0 us
  other arithmetic: 155 us -> 47.8 us
  matrix products: 185 us -> 111 us
  starting transfers between devices: 29.4 us -> 81.7 us
  local copies, waits for them, and re-layouts: 17.5 us -> 48.4 us
    reduce_scatter x2 -> x1, waiting for transfers between devices: 972 us -> 0.01 us  [shards(): lax.psum_scatter(mlp_term, ('z', 'x'), scatter_dimension=0, tiled=True)]
    unnamed x2 -> x0, blocking collectives: 651 us -> none
    ppermute x0 -> x61, waiting for transfers between devices: none -> 219 us  [the longest x47 171 us: ring_send(): lax.ppermute(values, axis, [(i, (i + shift) % size) for i in range(size)])]
    concatenate x3 -> x11, other arithmetic: 118 us -> 9.5 us  [the longest x1 4.86 us: shards(): jnp.concatenate([dot_tn(second_all, d_gate_up).astype(bf16), dot_tn(dy_al...]
    ppermute x0 -> x61, starting transfers between devices: none -> 81.6 us  [the longest x47 60.7 us: ring_send(): lax.ppermute(values, axis, [(i, (i + shift) % size) for i in range(size)])]
    dot_general x18 -> x32, matrix products: 185 us -> 111 us  [the longest x22 60.1 us: dot(): return jnp.dot(a, b, preferred_element_type=f32)]
    all_gather x2 -> x1, waiting for transfers between devices: 39.2 us -> 0.01 us  [shards(): mlp_w = lax.all_gather(mlp_rows_own, ('z', 'x'), axis=0, tiled=True)]
    all_to_all x8 -> x0, starting transfers between devices: 29 us -> none  [the longest x1 4.07 us: shards(): lax.all_to_all(d_values, 'seq', split_axis=0, concat_axis=1, tiled=True)]
  transfers between devices with their start and end apart: 13 -> 63, of which waited for: 9 -> 34; matrix products, arithmetic and copies ran while one was open for 12% -> 25% of each run, Pallas kernels for 0% -> 1%
where the time goes in v1:
time: 539 us; the launch traced here: 529 us
  waiting for transfers between devices  220 us (41%)
  matrix products  111 us (21%)
  starting transfers between devices  81.7 us (15%)
  local copies, waits for them, and re-layouts  48.4 us (9%)
  other arithmetic  47.8 us (9%)
  between operations  16.3 us (3%)
    ppermute x47, waiting for transfers between devices, ring_send(): lax.ppermute(values, axis, [(i, (i + shift) % size) for i in range(size)])  171 us
    ppermute x47, starting transfers between devices, ring_send(): lax.ppermute(values, axis, [(i, (i + shift) % size) for i in range(size)])  60.7 us
    dot_general x22, matrix products, dot(): return jnp.dot(a, b, preferred_element_type=f32)  60.1 us
    ppermute x12, waiting for transfers between devices, y_send(): lax.ppermute(values, ('seq', 'yh'), [(place(i), place((i + shift) % 4)) f...  47.5 us
    dot_general x5, matrix products, dot_nt(): return lax.dot_general(a, b, contract_cols, preferred_element_type=f32)  31.7 us
    unnamed x224, local copies, waits for them, and re-layouts  28.7 us
    dot_general x5, matrix products, dot_tn(): return lax.dot_general(a, b, contract_rows, preferred_element_type=f32)  19.1 us
    ppermute x12, starting transfers between devices, y_send(): lax.ppermute(values, ('seq', 'yh'), [(place(i), place((i + shift) % 4)) f...  11.6 us
  transfers between devices with their start and end apart: 63, of which 34 were waited for; matrix products, arithmetic and copies ran while one was open for 25% of the time, Pallas kernels for 1%

profile of v1, /device:TPU:1, one launch (start us, length us, event | category | flops | bytes accessed | tf_op | source)
XLA Modules:
  0.0 529.4 jit_solution(11363043166229594621)
XLA Ops:
  10.3 3.3 collective-permute-start.2
  18.2 3.8 collective-permute-start.24
  29.9 5.2 fusion.21
  41.2 2.9 collective-permute-start.11
  45.4 3.7 fusion.20
  59.1 3.2 collective-permute-start.13
  64.6 10.7 %collective-permute-done.4 = bf16[96,1152]{1,0:T(8,128)(2,1)S(1)} collective-permute-done((bf16[96,1152]{1,0:T(8,128)(2,1)S(1)}, bf16[96,1152]{1,0:T(8,128)(2,1)S(1)}, u32[]{:S(2)}, u32[]{:S(2)}) %collective-permute-start.4) | collective-permute-done | bytes 221216 | tf_op jit(solution)/shard_map/ppermute | solution.py:54
  78.5 3.3 collective-permute-start.7
  81.8 3.5 collective-permute-start.6
  86.3 6.1 %collective-permute-done.5 = bf16[192,1152]{1,0:T(8,128)(2,1)S(1)} collective-permute-done((bf16[192,1152]{1,0:T(8,128)(2,1)}, bf16[192,1152]{1,0:T(8,128)(2,1)S(1)}, u32[]{:S(2)}, u32[]{:S(2)}) %collective-permute-start.5) | collective-permute-done | bytes 442400 | tf_op jit(solution)/shard_map/ppermute | solution.py:54
  92.4 3.9 collective-permute-start.16
  97.3 21.5 %collective-permute-done.6 = bf16[192,1152]{1,0:T(8,128)(2,1)S(1)} collective-permute-done((bf16[192,1152]{1,0:T(8,128)(2,1)}, bf16[192,1152]{1,0:T(8,128)(2,1)S(1)}, u32[]{:S(2)}, u32[]{:S(2)}) %collective-permute-start.6) | collective-permute-done | bytes 442400 | tf_op jit(solution)/shard_map/ppermute | solution.py:54
  122.3 7.2 %collective-permute-start.8 = (bf16[768,1152]{1,0:T(8,128)(2,1)}, bf16[768,1152]{1,0:T(8,128)(2,1)S(1)}, u32[]{:S(2)}, u32[]{:S(2)}) collective-permute-start(bf16[768,1152]{1,0:T(8,128)(2,1)} %get-tuple-element.90), channel_id=1, source_target_pairs={{0,1},{1,0},{2,3},{3,2},{4,5},{5,4},{6,7},{7,6},{8,9},{9,8},{10,11... | collective-permute-start | bytes 5308424 | tf_op jit(solution)/shard_map/ppermute | solution.py:54
  132.5 28.5 %collective-permute-done.14 = bf16[192,1536]{1,0:T(8,128)(2,1)S(1)} collective-permute-done((bf16[192,1536]{1,0:T(8,128)(2,1)}, bf16[192,1536]{1,0:T(8,128)(2,1)S(1)}, u32[]{:S(2)}, u32[]{:S(2)}) %collective-permute-start.14) | collective-permute-done | bytes 589856 | tf_op jit(solution)/shard_map/ppermute | solution.py:54
  162.1 5.7 %collective-permute-done.15 = bf16[192,1536]{1,0:T(8,128)(2,1)S(1)} collective-permute-done((bf16[192,1536]{1,0:T(8,128)(2,1)}, bf16[192,1536]{1,0:T(8,128)(2,1)S(1)}, u32[]{:S(2)}, u32[]{:S(2)}) %collective-permute-start.15) | collective-permute-done | bytes 589856 | tf_op jit(solution)/shard_map/ppermute | solution.py:54
  176.4 3.3 fusion.42.qkv_ref
  185.4 3.2 collective-permute-done.9
  190.2 3.4 constant_dynamic-update-slice_fusion.35
  193.6 3.2 multiply_reduce_fusion.5
  201.6 7.5 %collective-permute-done.20 = bf16[128,1536]{1,0:T(8,128)(2,1)S(1)} collective-permute-done((bf16[128,1536]{1,0:T(8,128)(2,1)S(1)}, bf16[128,1536]{1,0:T(8,128)(2,1)S(1)}, u32[]{:S(2)}, u32[]{:S(2)}) %collective-permute-start.20) | collective-permute-done | bytes 393248 | tf_op jit(solution)/shard_map/ppermute | solution.py:59
  209.2 8.7 %collective-permute-done.19 = bf16[128,1536]{1,0:T(8,128)(2,1)S(1)} collective-permute-done((bf16[128,1536]{1,0:T(8,128)(2,1)S(1)}, bf16[128,1536]{1,0:T(8,128)(2,1)S(1)}, u32[]{:S(2)}, u32[]{:S(2)}) %collective-permute-start.19) | collective-permute-done | bytes 393248 | tf_op jit(solution)/shard_map/ppermute | solution.py:59
  225.8 13.5 %fusion.30 = f32[1024,2304]{1,0:T(8,128)} fusion(bf16[1024,1536]{1,0:T(8,128)(2,1)} %constant_dynamic-update-slice_fusion.44, bf16[1536,3456]{1,0:T(8,128)(2,1)} %all-gather.2.cloned.1.call-done), kind=kOutput, calls=%fused_computation.77 | convolution fusion | flops 7247757312 | bytes 19660800 | tf_op jit(solution)/shard_map/dot_general | solution.py:35
  239.3 9.2 %multiply_convert_fusion.1 = (bf16[1024,1152]{1,0:T(8,128)(2,1)S(1)}, bf16[1024,1152]{1,0:T(8,128)(2,1)S(1)}, bf16[1024,1152]{1,0:T(8,128)(2,1)S(1)}) fusion(f32[1024,2304]{1,0:T(8,128)} %fusion.30, bf16[1024,1536]{1,0:T(8,128)(2,1)S(1)} %copy-done.92, bf16[1536,3456]{1,0:T(8,128)(2,1)} %all-gather.2.cloned.1.call-done), kind=kOutput, calls=%fused_computation.83 | convolution fusion | flops 3641573376 | bytes 23199744 | tf_op jit(solution)/shard_map/dot_general | solution.py:35
  248.5 4.6 convolution_convert_fusion.1
  253.1 10.2 %convolution_convert_fusion = bf16[1536,2304]{1,0:T(8,128)(2,1)S(1)} fusion(bf16[1024,1536]{1,0:T(8,128)(2,1)} %constant_dynamic-update-slice_fusion.44, bf16[1024,1152]{1,0:T(8,128)(2,1)S(1)} %get-tuple-element.52, bf16[1024,1152]{1,0:T(8,128)(2,1)S(1)} %get-tuple-element.51), kind=kOutput, calls=%fused_computation.41 | convolution fusion | flops 7260733440 | bytes 14942208 | tf_op jit(solution)/shard_map/dot_general | solution.py:39
  263.3 11.6 %fusion.28 = f32[1024,1536]{1,0:T(8,128)S(1)} fusion(bf16[1536,3456]{1,0:T(8,128)(2,1)} %all-gather.2.cloned.1.call-done, bf16[1024,1152]{1,0:T(8,128)(2,1)} %copy-done.98, bf16[1024,1152]{1,0:T(8,128)(2,1)} %copy-done.97), kind=kOutput, calls=%fused_computation.75 | convolution fusion | flops 7257194496 | bytes 18087936 | tf_op jit(solution)/shard_map/dot_general | solution.py:43
  279.0 4.9 pad_maximum_fusion
  283.9 7.0 %fusion.38 = f32[1024,1536]{1,0:T(8,128)S(1)} fusion(bf16[1024,1152]{1,0:T(8,128)(2,1)} %copy-done.99, bf16[1536,3456]{1,0:T(8,128)(2,1)} %all-gather.2.cloned.1.call-done), kind=kOutput, calls=%fused_computation.98 | convolution fusion | flops 3623878656 | bytes 12189696 | tf_op jit(solution)/shard_map/dot_general | solution.py:43
  295.9 3.1 fusion.147
  302.1 4.2 fusion.148
  306.3 11.7 %collective-permute-done.34 = bf16[128,1536]{1,0:T(8,128)(2,1)S(1)} collective-permute-done((bf16[128,1536]{1,0:T(8,128)(2,1)S(1)}, bf16[128,1536]{1,0:T(8,128)(2,1)S(1)}, u32[]{:S(2)}, u32[]{:S(2)}) %collective-permute-start.34) | collective-permute-done | bytes 393248 | tf_op jit(solution)/shard_map/ppermute | solution.py:59
  318.0 4.3 collective-permute-done.35
  323.8 7.3 %convolution_convert_fusion.2 = bf16[128,1536]{1,0:T(8,128)(2,1)} fusion(pred[1536,1536]{1,0:T(32,128)(4,1)} %fusion.21, bf16[128,1536]{1,0:T(8,128)(2,1)} %fusion.135, bf16[1536,1536]{1,0:T(8,128)(2,1)} %constant_dynamic-update-slice_fusion.35), kind=kOutput, calls=%fused_computation.114 | convolution fusion | flops 1208352768 | bytes 7864320 | tf_op jit(solution)/shard_map/dot_general | solution.py:43
  332.5 3.0 convolution_reduce_fusion
  362.5 10.0 %collective-permute-done.27 = bf16[128,1536]{1,0:T(8,128)(2,1)S(1)} collective-permute-done((bf16[128,1536]{1,0:T(8,128)(2,1)S(1)}, bf16[128,1536]{1,0:T(8,128)(2,1)S(1)}, u32[]{:S(2)}, u32[]{:S(2)}) %collective-permute-start.27) | collective-permute-done | bytes 393248 | tf_op jit(solution)/shard_map/ppermute | solution.py:59
  372.5 3.7 fusion.47
  380.0 6.7 %collective-permute-done.38 = bf16[128,1536]{1,0:T(8,128)(2,1)S(1)} collective-permute-done((bf16[128,1536]{1,0:T(8,128)(2,1)S(1)}, bf16[128,1536]{1,0:T(8,128)(2,1)S(1)}, u32[]{:S(2)}, u32[]{:S(2)}) %collective-permute-start.38) | collective-permute-done | bytes 393248 | tf_op jit(solution)/shard_map/ppermute | solution.py:54
  394.3 6.3 %collective-permute-done.40 = bf16[192,1152]{1,0:T(8,128)(2,1)S(1)} collective-permute-done((bf16[192,1152]{1,0:T(8,128)(2,1)S(1)}, bf16[192,1152]{1,0:T(8,128)(2,1)S(1)}, u32[]{:S(2)}, u32[]{:S(2)}) %collective-permute-start.40) | collective-permute-done | bytes 442400 | tf_op jit(solution)/shard_map/ppermute | solution.py:54
  403.5 11.0 %collective-permute-done.41 = bf16[192,1152]{1,0:T(8,128)(2,1)S(1)} collective-permute-done((bf16[192,1152]{1,0:T(8,128)(2,1)S(1)}, bf16[192,1152]{1,0:T(8,128)(2,1)S(1)}, u32[]{:S(2)}, u32[]{:S(2)}) %collective-permute-start.41) | collective-permute-done | bytes 442400 | tf_op jit(solution)/shard_map/ppermute | solution.py:54
  418.7 3.8 collective-permute-done.43
  426.5 3.1 collective-permute-done.46
  433.0 8.8 %collective-permute-done.49 = bf16[192,1536]{1,0:T(8,128)(2,1)S(1)} collective-permute-done((bf16[192,1536]{1,0:T(8,128)(2,1)S(1)}, bf16[192,1536]{1,0:T(8,128)(2,1)S(1)}, u32[]{:S(2)}, u32[]{:S(2)}) %collective-permute-start.49) | collective-permute-done | bytes 589856 | tf_op jit(solution)/shard_map/ppermute | solution.py:54
  443.5 16.2 %collective-permute-done.50 = bf16[192,1536]{1,0:T(8,128)(2,1)S(1)} collective-permute-done((bf16[192,1536]{1,0:T(8,128)(2,1)S(1)}, bf16[192,1536]{1,0:T(8,128)(2,1)S(1)}, u32[]{:S(2)}, u32[]{:S(2)}) %collective-permute-start.50) | collective-permute-done | bytes 589856 | tf_op jit(solution)/shard_map/ppermute | solution.py:54
  461.4 8.1 %collective-permute-done.52 = bf16[96,1536]{1,0:T(8,128)(2,1)S(1)} collective-permute-done((bf16[96,1536]{1,0:T(8,128)(2,1)S(1)}, bf16[96,1536]{1,0:T(8,128)(2,1)S(1)}, u32[]{:S(2)}, u32[]{:S(2)}) %collective-permute-start.52) | collective-permute-done | bytes 294944 | tf_op jit(solution)/shard_map/ppermute | solution.py:54
  481.7 5.5 %collective-permute-start.59 = (bf16[24,3456]{1,0:T(8,128)(2,1)S(1)}, bf16[24,3456]{1,0:T(8,128)(2,1)S(1)}, u32[]{:S(2)}, u32[]{:S(2)}) collective-permute-start(bf16[24,3456]{1,0:T(8,128)(2,1)S(1)} %get-tuple-element.73), channel_id=1, source_target_pairs={{0,9},{1,8},{8,1},{9,0},{2,11},{3,10},{10,3},{11,2},{4,13},{5,12},... | collective-permute-start | bytes 497672 | tf_op jit(solution)/shard_map/ppermute | solution.py:65
  491.3 4.3 collective-permute-done.58
  498.2 14.4 %collective-permute-done.60 = bf16[4,24,3456]{2,1,0:T(8,128)(2,1)S(1)} collective-permute-done((bf16[4,24,3456]{2,1,0:T(8,128)(2,1)S(1)}, bf16[4,24,3456]{2,1,0:T(8,128)(2,1)S(1)}, u32[]{:S(2)}, u32[]{:S(2)}) %collective-permute-start.60) | collective-permute-done | bytes 663584 | tf_op jit(solution)/shard_map/ppermute | solution.py:54
  517.9 4.5 multiply_subtract_fusion
  (458 shorter events, 170.4 us)
Async XLA Ops:
  7.2 218.6 %all-gather.2.cloned.1.call-start = ((), (), s32[]{:S(2)}) async-start(), calls=%async_computation.1 | async-start | bytes 11280384 | tf_op jit(solution)/shard_map/all_gather | solution.py:295
  10.3 40.3 %collective-permute-start.2 = (bf16[24,1152]{1,0:T(8,128)(2,1)}, bf16[24,1152]{1,0:T(8,128)(2,1)S(1)}, u32[]{:S(2)}, u32[]{:S(2)}) collective-permute-start(bf16[24,1152]{1,0:T(8,128)(2,1)} %get-tuple-element.140), channel_id=1, source_target_pairs={{0,6},{2,0},{4,2},{6,4},{1,7},{3,1},{5,3},{7,5},{8,14},{10,8},{12,... | collective-permute-start | bytes 165896 | tf_op jit(solution)/shard_map/ppermute | solution.py:54
  13.6 36.0 %collective-permute-start.1 = (bf16[24,1152]{1,0:T(8,128)(2,1)}, bf16[24,1152]{1,0:T(8,128)(2,1)S(1)}, u32[]{:S(2)}, u32[]{:S(2)}) collective-permute-start(bf16[24,1152]{1,0:T(8,128)(2,1)} %get-tuple-element.140), channel_id=1, source_target_pairs={{0,2},{2,4},{4,6},{6,0},{1,3},{3,5},{5,7},{7,1},{8,10},{10,12},{12... | collective-permute-start | bytes 165896 | tf_op jit(solution)/shard_map/ppermute | solution.py:54
  18.2 19.9 %collective-permute-start.24 = (bf16[24,3456]{1,0:T(8,128)(2,1)S(1)}, bf16[24,3456]{1,0:T(8,128)(2,1)S(1)}, u32[]{:S(2)}, u32[]{:S(2)}) collective-permute-start(bf16[24,3456]{1,0:T(8,128)(2,1)S(1)} %get-tuple-element.81), channel_id=1, source_target_pairs={{0,9},{1,8},{8,1},{9,0},{2,11},{3,10},{10,3},{11,2},{4,13},{5,12},... | collective-permute-start | bytes 497672 | tf_op jit(solution)/shard_map/ppermute | solution.py:65
  22.1 18.1 %collective-permute-start.23 = (bf16[24,3456]{1,0:T(8,128)(2,1)S(1)}, bf16[24,3456]{1,0:T(8,128)(2,1)S(1)}, u32[]{:S(2)}, u32[]{:S(2)}) collective-permute-start(bf16[24,3456]{1,0:T(8,128)(2,1)S(1)} %get-tuple-element.82), channel_id=1, source_target_pairs={{0,8},{8,0},{1,9},{9,1},{2,10},{10,2},{3,11},{11,3},{4,12},{12,4},... | collective-permute-start | bytes 497672 | tf_op jit(solution)/shard_map/ppermute | solution.py:54
  22.1 19.0 %collective-permute-start.22 = (bf16[24,3456]{1,0:T(8,128)(2,1)S(1)}, bf16[24,3456]{1,0:T(8,128)(2,1)S(1)}, u32[]{:S(2)}, u32[]{:S(2)}) collective-permute-start(bf16[24,3456]{1,0:T(8,128)(2,1)S(1)} %get-tuple-element.83), channel_id=1, source_target_pairs={{0,1},{1,0},{2,3},{3,2},{4,5},{5,4},{6,7},{7,6},{8,9},{9,8},{10,11... | collective-permute-start | bytes 497672 | tf_op jit(solution)/shard_map/ppermute | solution.py:54
  38.1 14.0 %collective-permute-start.3 = (bf16[24,1152]{1,0:T(8,128)(2,1)}, bf16[24,1152]{1,0:T(8,128)(2,1)S(1)}, u32[]{:S(2)}, u32[]{:S(2)}) collective-permute-start(bf16[24,1152]{1,0:T(8,128)(2,1)} %get-tuple-element.140), channel_id=1, source_target_pairs={{0,4},{2,6},{4,0},{6,2},{1,5},{3,7},{5,1},{7,3},{8,12},{10,14},{12... | collective-permute-start | bytes 165896 | tf_op jit(solution)/shard_map/ppermute | solution.py:54
  40.2 17.7 %collective-permute-start.12 = (bf16[24,1536]{1,0:T(8,128)(2,1)}, bf16[24,1536]{1,0:T(8,128)(2,1)S(1)}, u32[]{:S(2)}, u32[]{:S(2)}) collective-permute-start(bf16[24,1536]{1,0:T(8,128)(2,1)} %get-tuple-element.148), channel_id=1, source_target_pairs={{0,4},{2,6},{4,0},{6,2},{1,5},{3,7},{5,1},{7,3},{8,12},{10,14},{12... | collective-permute-start | bytes 221192 | tf_op jit(solution)/shard_map/ppermute | solution.py:54
  41.2 17.0 %collective-permute-start.11 = (bf16[24,1536]{1,0:T(8,128)(2,1)}, bf16[24,1536]{1,0:T(8,128)(2,1)}, u32[]{:S(2)}, u32[]{:S(2)}) collective-permute-start(bf16[24,1536]{1,0:T(8,128)(2,1)} %get-tuple-element.148), channel_id=1, source_target_pairs={{0,6},{2,0},{4,2},{6,4},{1,7},{3,1},{5,3},{7,5},{8,14},{10,8},{12,... | collective-permute-start | bytes 221192 | tf_op jit(solution)/shard_map/ppermute | solution.py:54
  45.2 435.2 %reduce-scatter.2.cloned.1.call-start = ((), (), s32[]{:S(2)}) async-start(), calls=%async_computation.2 | async-start | bytes 11280384 | tf_op jit(solution)/shard_map/reduce_scatter | solution.py:345
  49.6 8.5 %collective-permute-start.10 = (bf16[24,1536]{1,0:T(8,128)(2,1)}, bf16[24,1536]{1,0:T(8,128)(2,1)S(1)}, u32[]{:S(2)}, u32[]{:S(2)}) collective-permute-start(bf16[24,1536]{1,0:T(8,128)(2,1)} %get-tuple-element.148), channel_id=1, source_target_pairs={{0,2},{2,4},{4,6},{6,0},{1,3},{3,5},{5,7},{7,1},{8,10},{10,12},{12... | collective-permute-start | bytes 221192 | tf_op jit(solution)/shard_map/ppermute | solution.py:54
  50.6 71.7 %collective-permute-start = (bf16[128,1536]{1,0:T(8,128)(2,1)}, bf16[128,1536]{1,0:T(8,128)(2,1)S(1)}, u32[]{:S(2)}, u32[]{:S(2)}) collective-permute-start(bf16[128,1536]{1,0:T(8,128)(2,1)} %bitcast.120), channel_id=1, source_target_pairs={{0,64},{64,0},{1,65},{65,1},{2,66},{66,2},{3,67},{67,3},{4,68},{68... | collective-permute-start | bytes 1179656 | tf_op jit(solution)/shard_map/ppermute | solution.py:54
  52.8 129.5 %collective-permute-start.31 = (bf16[128,1536]{1,0:T(8,128)(2,1)S(1)}, bf16[128,1536]{1,0:T(8,128)(2,1)S(1)}, u32[]{:S(2)}, u32[]{:S(2)}) collective-permute-start(bf16[128,1536]{1,0:T(8,128)(2,1)S(1)} %get-tuple-element.150), channel_id=1, source_target_pairs={{0,8},{64,72},{8,0},{72,64},{1,9},{65,73},{9,1},{73,65},{2,10},{66... | collective-permute-start | bytes 1179656 | tf_op jit(solution)/shard_map/ppermute | solution.py:59
  57.8 17.4 %collective-permute-start.4 = (bf16[96,1152]{1,0:T(8,128)(2,1)S(1)}, bf16[96,1152]{1,0:T(8,128)(2,1)S(1)}, u32[]{:S(2)}, u32[]{:S(2)}) collective-permute-start(bf16[96,1152]{1,0:T(8,128)(2,1)S(1)} %pad_maximum_fusion.14), channel_id=1, source_target_pairs={{0,8},{8,0},{1,9},{9,1},{2,10},{10,2},{3,11},{11,3},{4,12},{12,4},... | collective-permute-start | bytes 663560 | tf_op jit(solution)/shard_map/ppermute | solution.py:54
  59.1 22.7 %collective-permute-start.13 = (bf16[96,1536]{1,0:T(8,128)(2,1)S(1)}, bf16[96,1536]{1,0:T(8,128)(2,1)S(1)}, u32[]{:S(2)}, u32[]{:S(2)}) collective-permute-start(bf16[96,1536]{1,0:T(8,128)(2,1)S(1)} %pad_maximum_fusion.13), channel_id=1, source_target_pairs={{0,8},{8,0},{1,9},{9,1},{2,10},{10,2},{3,11},{11,3},{4,12},{12,4},... | collective-permute-start | bytes 884744 | tf_op jit(solution)/shard_map/ppermute | solution.py:54
  76.2 16.3 %collective-permute-start.5 = (bf16[192,1152]{1,0:T(8,128)(2,1)}, bf16[192,1152]{1,0:T(8,128)(2,1)S(1)}, u32[]{:S(2)}, u32[]{:S(2)}) collective-permute-start(bf16[192,1152]{1,0:T(8,128)(2,1)} %get-tuple-element.111), channel_id=1, source_target_pairs={{0,16},{16,32},{32,48},{48,0},{1,17},{17,33},{33,49},{49,1},{2,18}... | collective-permute-start | bytes 1327112 | tf_op jit(solution)/shard_map/ppermute | solution.py:54
  78.5 41.9 %collective-permute-start.7 = (bf16[192,1152]{1,0:T(8,128)(2,1)}, bf16[192,1152]{1,0:T(8,128)(2,1)S(1)}, u32[]{:S(2)}, u32[]{:S(2)}) collective-permute-start(bf16[192,1152]{1,0:T(8,128)(2,1)} %get-tuple-element.111), channel_id=1, source_target_pairs={{0,32},{16,48},{32,0},{48,16},{1,33},{17,49},{33,1},{49,17},{2,34}... | collective-permute-start | bytes 1327112 | tf_op jit(solution)/shard_map/ppermute | solution.py:54
  81.8 37.0 %collective-permute-start.6 = (bf16[192,1152]{1,0:T(8,128)(2,1)}, bf16[192,1152]{1,0:T(8,128)(2,1)S(1)}, u32[]{:S(2)}, u32[]{:S(2)}) collective-permute-start(bf16[192,1152]{1,0:T(8,128)(2,1)} %get-tuple-element.111), channel_id=1, source_target_pairs={{0,48},{16,0},{32,16},{48,32},{1,49},{17,1},{33,17},{49,33},{2,50}... | collective-permute-start | bytes 1327112 | tf_op jit(solution)/shard_map/ppermute | solution.py:54
  92.4 76.6 %collective-permute-start.16 = (bf16[192,1536]{1,0:T(8,128)(2,1)}, bf16[192,1536]{1,0:T(8,128)(2,1)S(1)}, u32[]{:S(2)}, u32[]{:S(2)}) collective-permute-start(bf16[192,1536]{1,0:T(8,128)(2,1)} %get-tuple-element.105), channel_id=1, source_target_pairs={{0,32},{16,48},{32,0},{48,16},{1,33},{17,49},{33,1},{49,17},{2,34}... | collective-permute-start | bytes 1769480 | tf_op jit(solution)/shard_map/ppermute | solution.py:54
  118.8 49.0 %collective-permute-start.15 = (bf16[192,1536]{1,0:T(8,128)(2,1)}, bf16[192,1536]{1,0:T(8,128)(2,1)S(1)}, u32[]{:S(2)}, u32[]{:S(2)}) collective-permute-start(bf16[192,1536]{1,0:T(8,128)(2,1)} %get-tuple-element.105), channel_id=1, source_target_pairs={{0,48},{16,0},{32,16},{48,32},{1,49},{17,1},{33,17},{49,33},{2,50}... | collective-permute-start | bytes 1769480 | tf_op jit(solution)/shard_map/ppermute | solution.py:54
  120.4 40.6 %collective-permute-start.14 = (bf16[192,1536]{1,0:T(8,128)(2,1)}, bf16[192,1536]{1,0:T(8,128)(2,1)S(1)}, u32[]{:S(2)}, u32[]{:S(2)}) collective-permute-start(bf16[192,1536]{1,0:T(8,128)(2,1)} %get-tuple-element.105), channel_id=1, source_target_pairs={{0,16},{16,32},{32,48},{48,0},{1,17},{17,33},{33,49},{49,1},{2,18}... | collective-permute-start | bytes 1769480 | tf_op jit(solution)/shard_map/ppermute | solution.py:54
  122.3 50.1 %collective-permute-start.8 = (bf16[768,1152]{1,0:T(8,128)(2,1)}, bf16[768,1152]{1,0:T(8,128)(2,1)S(1)}, u32[]{:S(2)}, u32[]{:S(2)}) collective-permute-start(bf16[768,1152]{1,0:T(8,128)(2,1)} %get-tuple-element.90), channel_id=1, source_target_pairs={{0,1},{1,0},{2,3},{3,2},{4,5},{5,4},{6,7},{7,6},{8,9},{9,8},{10,11... | collective-permute-start | bytes 5308424 | tf_op jit(solution)/shard_map/ppermute | solution.py:54
  161.0 21.3 %collective-permute-start.30 = (bf16[128,1536]{1,0:T(8,128)(2,1)S(1)}, bf16[128,1536]{1,0:T(8,128)(2,1)}, u32[]{:S(2)}, u32[]{:S(2)}) collective-permute-start(bf16[128,1536]{1,0:T(8,128)(2,1)S(1)} %get-tuple-element.150), channel_id=1, source_target_pairs={{0,72},{64,0},{8,64},{72,8},{1,73},{65,1},{9,65},{73,9},{2,74},{66... | collective-permute-start | bytes 1179656 | tf_op jit(solution)/shard_map/ppermute | solution.py:59
  167.8 14.4 %collective-permute-start.29 = (bf16[128,1536]{1,0:T(8,128)(2,1)S(1)}, bf16[128,1536]{1,0:T(8,128)(2,1)}, u32[]{:S(2)}, u32[]{:S(2)}) collective-permute-start(bf16[128,1536]{1,0:T(8,128)(2,1)S(1)} %get-tuple-element.150), channel_id=1, source_target_pairs={{0,64},{64,8},{8,72},{72,0},{1,65},{65,9},{9,73},{73,1},{2,66},{66... | collective-permute-start | bytes 1179656 | tf_op jit(solution)/shard_map/ppermute | solution.py:59
  170.1 20.1 %collective-permute-start.17 = (bf16[768,1536]{1,0:T(8,128)(2,1)}, bf16[768,1536]{1,0:T(8,128)(2,1)}, u32[]{:S(2)}, u32[]{:S(2)}) collective-permute-start(bf16[768,1536]{1,0:T(8,128)(2,1)} %get-tuple-element.84), channel_id=1, source_target_pairs={{0,1},{1,0},{2,3},{3,2},{4,5},{5,4},{6,7},{7,6},{8,9},{9,8},{10,11... | collective-permute-start | bytes 7077896 | tf_op jit(solution)/shard_map/ppermute | solution.py:54
  183.6 38.1 %collective-permute-start.32 = (bf16[512,1536]{1,0:T(8,128)(2,1)S(1)}, bf16[512,1536]{1,0:T(8,128)(2,1)S(1)}, u32[]{:S(2)}, u32[]{:S(2)}) collective-permute-start(bf16[512,1536]{1,0:T(8,128)(2,1)S(1)} %pad_maximum_fusion.6), channel_id=1, source_target_pairs={{0,1},{1,0},{2,3},{3,2},{4,5},{5,4},{6,7},{7,6},{8,9},{9,8},{10,11... | collective-permute-start | bytes 4718600 | tf_op jit(solution)/shard_map/ppermute | solution.py:54
  197.8 11.4 %collective-permute-start.20 = (bf16[128,1536]{1,0:T(8,128)(2,1)S(1)}, bf16[128,1536]{1,0:T(8,128)(2,1)S(1)}, u32[]{:S(2)}, u32[]{:S(2)}) collective-permute-start(bf16[128,1536]{1,0:T(8,128)(2,1)S(1)} %get-tuple-element.50), channel_id=1, source_target_pairs={{0,8},{64,72},{8,0},{72,64},{1,9},{65,73},{9,1},{73,65},{2,10},{66... | collective-permute-start | bytes 1179656 | tf_op jit(solution)/shard_map/ppermute | solution.py:59
  200.1 17.7 %collective-permute-start.19 = (bf16[128,1536]{1,0:T(8,128)(2,1)S(1)}, bf16[128,1536]{1,0:T(8,128)(2,1)S(1)}, u32[]{:S(2)}, u32[]{:S(2)}) collective-permute-start(bf16[128,1536]{1,0:T(8,128)(2,1)S(1)} %get-tuple-element.50), channel_id=1, source_target_pairs={{0,72},{64,0},{8,64},{72,8},{1,73},{65,1},{9,65},{73,9},{2,74},{66... | collective-permute-start | bytes 1179656 | tf_op jit(solution)/shard_map/ppermute | solution.py:59
  200.3 18.4 %collective-permute-start.18 = (bf16[128,1536]{1,0:T(8,128)(2,1)S(1)}, bf16[128,1536]{1,0:T(8,128)(2,1)S(1)}, u32[]{:S(2)}, u32[]{:S(2)}) collective-permute-start(bf16[128,1536]{1,0:T(8,128)(2,1)S(1)} %get-tuple-element.50), channel_id=1, source_target_pairs={{0,64},{64,8},{8,72},{72,0},{1,65},{65,9},{9,73},{73,1},{2,66},{66... | collective-permute-start | bytes 1179656 | tf_op jit(solution)/shard_map/ppermute | solution.py:59
  279.0 16.9 %collective-permute-start.33 = (bf16[512,1536]{1,0:T(8,128)(2,1)}, bf16[512,1536]{1,0:T(8,128)(2,1)}, u32[]{:S(2)}, u32[]{:S(2)}) collective-permute-start(bf16[512,1536]{1,0:T(8,128)(2,1)} %slice.494), channel_id=1, source_target_pairs={{0,1},{1,0},{2,3},{3,2},{4,5},{5,4},{6,7},{7,6},{8,9},{9,8},{10,11... | collective-permute-start | bytes 4718600 | tf_op jit(solution)/shard_map/ppermute | solution.py:54
  299.0 18.9 %collective-permute-start.34 = (bf16[128,1536]{1,0:T(8,128)(2,1)S(1)}, bf16[128,1536]{1,0:T(8,128)(2,1)S(1)}, u32[]{:S(2)}, u32[]{:S(2)}) collective-permute-start(bf16[128,1536]{1,0:T(8,128)(2,1)S(1)} %get-tuple-element.60), channel_id=1, source_target_pairs={{0,72},{64,0},{8,64},{72,8},{1,73},{65,1},{9,65},{73,9},{2,74},{66... | collective-permute-start | bytes 1179656 | tf_op jit(solution)/shard_map/ppermute | solution.py:59
  301.2 16.8 %collective-permute-start.36 = (bf16[128,1536]{1,0:T(8,128)(2,1)S(1)}, bf16[128,1536]{1,0:T(8,128)(2,1)S(1)}, u32[]{:S(2)}, u32[]{:S(2)}) collective-permute-start(bf16[128,1536]{1,0:T(8,128)(2,1)S(1)} %get-tuple-element.61), channel_id=1, source_target_pairs={{0,8},{64,72},{8,0},{72,64},{1,9},{65,73},{9,1},{73,65},{2,10},{66... | collective-permute-start | bytes 1179656 | tf_op jit(solution)/shard_map/ppermute | solution.py:59
  301.6 20.7 %collective-permute-start.35 = (bf16[128,1536]{1,0:T(8,128)(2,1)S(1)}, bf16[128,1536]{1,0:T(8,128)(2,1)S(1)}, u32[]{:S(2)}, u32[]{:S(2)}) collective-permute-start(bf16[128,1536]{1,0:T(8,128)(2,1)S(1)} %get-tuple-element.62), channel_id=1, source_target_pairs={{0,64},{64,8},{8,72},{72,0},{1,65},{65,9},{9,73},{73,1},{2,66},{66... | collective-permute-start | bytes 1179656 | tf_op jit(solution)/shard_map/ppermute | solution.py:59
  349.7 37.2 %collective-permute-start.39 = (bf16[768,1152]{1,0:T(8,128)(2,1)S(1)}, bf16[768,1152]{1,0:T(8,128)(2,1)}, u32[]{:S(2)}, u32[]{:S(2)}) collective-permute-start(bf16[768,1152]{1,0:T(8,128)(2,1)S(1)} %fusion.35), channel_id=1, source_target_pairs={{0,1},{1,0},{2,3},{3,2},{4,5},{5,4},{6,7},{7,6},{8,9},{9,8},{10,11... | collective-permute-start | bytes 5308424 | tf_op jit(solution)/shard_map/ppermute | solution.py:54
  351.3 9.7 %collective-permute-start.26 = (bf16[128,1536]{1,0:T(8,128)(2,1)S(1)}, bf16[128,1536]{1,0:T(8,128)(2,1)S(1)}, u32[]{:S(2)}, u32[]{:S(2)}) collective-permute-start(bf16[128,1536]{1,0:T(8,128)(2,1)S(1)} %get-tuple-element.63), channel_id=1, source_target_pairs={{0,72},{64,0},{8,64},{72,8},{1,73},{65,1},{9,65},{73,9},{2,74},{66... | collective-permute-start | bytes 1179656 | tf_op jit(solution)/shard_map/ppermute | solution.py:59
  351.3 11.2 %collective-permute-start.28 = (bf16[128,1536]{1,0:T(8,128)(2,1)S(1)}, bf16[128,1536]{1,0:T(8,128)(2,1)S(1)}, u32[]{:S(2)}, u32[]{:S(2)}) collective-permute-start(bf16[128,1536]{1,0:T(8,128)(2,1)S(1)} %get-tuple-element.64), channel_id=1, source_target_pairs={{0,8},{64,72},{8,0},{72,64},{1,9},{65,73},{9,1},{73,65},{2,10},{66... | collective-permute-start | bytes 1179656 | tf_op jit(solution)/shard_map/ppermute | solution.py:59
  353.1 19.4 %collective-permute-start.27 = (bf16[128,1536]{1,0:T(8,128)(2,1)S(1)}, bf16[128,1536]{1,0:T(8,128)(2,1)S(1)}, u32[]{:S(2)}, u32[]{:S(2)}) collective-permute-start(bf16[128,1536]{1,0:T(8,128)(2,1)S(1)} %get-tuple-element.65), channel_id=1, source_target_pairs={{0,64},{64,8},{8,72},{72,0},{1,65},{65,9},{9,73},{73,1},{2,66},{66... | collective-permute-start | bytes 1179656 | tf_op jit(solution)/shard_map/ppermute | solution.py:59
  356.4 69.2 %collective-permute-start.48 = (bf16[768,1536]{1,0:T(8,128)(2,1)}, bf16[768,1536]{1,0:T(8,128)(2,1)S(1)}, u32[]{:S(2)}, u32[]{:S(2)}) collective-permute-start(bf16[768,1536]{1,0:T(8,128)(2,1)} %slice.493), channel_id=1, source_target_pairs={{0,1},{1,0},{2,3},{3,2},{4,5},{5,4},{6,7},{7,6},{8,9},{9,8},{10,11... | collective-permute-start | bytes 7077896 | tf_op jit(solution)/shard_map/ppermute | solution.py:54
  376.3 10.4 %collective-permute-start.38 = (bf16[128,1536]{1,0:T(8,128)(2,1)S(1)}, bf16[128,1536]{1,0:T(8,128)(2,1)S(1)}, u32[]{:S(2)}, u32[]{:S(2)}) collective-permute-start(bf16[128,1536]{1,0:T(8,128)(2,1)S(1)} %slice.496), channel_id=1, source_target_pairs={{0,64},{64,0},{1,65},{65,1},{2,66},{66,2},{3,67},{67,3},{4,68},{68... | collective-permute-start | bytes 1179656 | tf_op jit(solution)/shard_map/ppermute | solution.py:54
  389.2 11.4 %collective-permute-start.40 = (bf16[192,1152]{1,0:T(8,128)(2,1)S(1)}, bf16[192,1152]{1,0:T(8,128)(2,1)S(1)}, u32[]{:S(2)}, u32[]{:S(2)}) collective-permute-start(bf16[192,1152]{1,0:T(8,128)(2,1)S(1)} %get-tuple-element.57), channel_id=1, source_target_pairs={{0,48},{16,0},{32,16},{48,32},{1,49},{17,1},{33,17},{49,33},{2,50}... | collective-permute-start | bytes 1327112 | tf_op jit(solution)/shard_map/ppermute | solution.py:54
  391.8 11.6 %collective-permute-start.42 = (bf16[192,1152]{1,0:T(8,128)(2,1)S(1)}, bf16[192,1152]{1,0:T(8,128)(2,1)S(1)}, u32[]{:S(2)}, u32[]{:S(2)}) collective-permute-start(bf16[192,1152]{1,0:T(8,128)(2,1)S(1)} %get-tuple-element.58), channel_id=1, source_target_pairs={{0,32},{16,48},{32,0},{48,16},{1,33},{17,49},{33,1},{49,17},{2,34}... | collective-permute-start | bytes 1327112 | tf_op jit(solution)/shard_map/ppermute | solution.py:54
  391.9 22.6 %collective-permute-start.41 = (bf16[192,1152]{1,0:T(8,128)(2,1)S(1)}, bf16[192,1152]{1,0:T(8,128)(2,1)S(1)}, u32[]{:S(2)}, u32[]{:S(2)}) collective-permute-start(bf16[192,1152]{1,0:T(8,128)(2,1)S(1)} %get-tuple-element.59), channel_id=1, source_target_pairs={{0,16},{16,32},{32,48},{48,0},{1,17},{17,33},{33,49},{49,1},{2,18}... | collective-permute-start | bytes 1327112 | tf_op jit(solution)/shard_map/ppermute | solution.py:54
  430.1 11.7 %collective-permute-start.49 = (bf16[192,1536]{1,0:T(8,128)(2,1)S(1)}, bf16[192,1536]{1,0:T(8,128)(2,1)S(1)}, u32[]{:S(2)}, u32[]{:S(2)}) collective-permute-start(bf16[192,1536]{1,0:T(8,128)(2,1)S(1)} %get-tuple-element.54), channel_id=1, source_target_pairs={{0,48},{16,0},{32,16},{48,32},{1,49},{17,1},{33,17},{49,33},{2,50}... | collective-permute-start | bytes 1769480 | tf_op jit(solution)/shard_map/ppermute | solution.py:54
  430.1 13.3 %collective-permute-start.51 = (bf16[192,1536]{1,0:T(8,128)(2,1)S(1)}, bf16[192,1536]{1,0:T(8,128)(2,1)S(1)}, u32[]{:S(2)}, u32[]{:S(2)}) collective-permute-start(bf16[192,1536]{1,0:T(8,128)(2,1)S(1)} %get-tuple-element.55), channel_id=1, source_target_pairs={{0,32},{16,48},{32,0},{48,16},{1,33},{17,49},{33,1},{49,17},{2,34}... | collective-permute-start | bytes 1769480 | tf_op jit(solution)/shard_map/ppermute | solution.py:54
  431.3 28.3 %collective-permute-start.50 = (bf16[192,1536]{1,0:T(8,128)(2,1)S(1)}, bf16[192,1536]{1,0:T(8,128)(2,1)S(1)}, u32[]{:S(2)}, u32[]{:S(2)}) collective-permute-start(bf16[192,1536]{1,0:T(8,128)(2,1)S(1)} %get-tuple-element.56), channel_id=1, source_target_pairs={{0,16},{16,32},{32,48},{48,0},{1,17},{17,33},{33,49},{49,1},{2,18}... | collective-permute-start | bytes 1769480 | tf_op jit(solution)/shard_map/ppermute | solution.py:54
  459.9 9.7 %collective-permute-start.52 = (bf16[96,1536]{1,0:T(8,128)(2,1)S(1)}, bf16[96,1536]{1,0:T(8,128)(2,1)S(1)}, u32[]{:S(2)}, u32[]{:S(2)}) collective-permute-start(bf16[96,1536]{1,0:T(8,128)(2,1)S(1)} %slice.497), channel_id=1, source_target_pairs={{0,8},{8,0},{1,9},{9,1},{2,10},{10,2},{3,11},{11,3},{4,12},{12,4},... | collective-permute-start | bytes 884744 | tf_op jit(solution)/shard_map/ppermute | solution.py:54
  481.7 9.6 %collective-permute-start.59 = (bf16[24,3456]{1,0:T(8,128)(2,1)S(1)}, bf16[24,3456]{1,0:T(8,128)(2,1)S(1)}, u32[]{:S(2)}, u32[]{:S(2)}) collective-permute-start(bf16[24,3456]{1,0:T(8,128)(2,1)S(1)} %get-tuple-element.73), channel_id=1, source_target_pairs={{0,9},{1,8},{8,1},{9,0},{2,11},{3,10},{10,3},{11,2},{4,13},{5,12},... | collective-permute-start | bytes 497672 | tf_op jit(solution)/shard_map/ppermute | solution.py:65
  495.9 16.8 %collective-permute-start.60 = (bf16[4,24,3456]{2,1,0:T(8,128)(2,1)S(1)}, bf16[4,24,3456]{2,1,0:T(8,128)(2,1)S(1)}, u32[]{:S(2)}, u32[]{:S(2)}) collective-permute-start(bf16[4,24,3456]{2,1,0:T(8,128)(2,1)S(1)} %pad_maximum_fusion.11), channel_id=1, source_target_pairs={{0,64},{64,0},{1,65},{65,1},{2,66},{66,2},{3,67},{67,3},{4,68},{68... | collective-permute-start | bytes 1990664 | tf_op jit(solution)/shard_map/ppermute | solution.py:54
  (115 other events, 1625.1 us)
Sparse Core Ops, SparseCore 0:
  45.4 123.2 all-gather.1
  284.0 89.6 reduce-scatter.1

commit v2 on v1

--- a/solution.py
+++ b/solution.py
@@ -61,8 +61,31 @@
     )
 
 
-def swap_both(values):
-    return lax.ppermute(values, ("yh", "core"), [(i, 3 - i) for i in range(4)])
+def cross_send(values):
+    return lax.ppermute(values, ("seq", "yh"), [(i, 3 - i) for i in range(4)])
+
+
+def core_send(values):
+    return ring_send(values, "core", 1)
+
+
+def seq_send(values):
+    return ring_send(values, "seq", 1)
+
+
+def hold_kernel(*refs):
+    pass
+
+
+def hold(values, *after):
+    anywhere = pl.BlockSpec(memory_space=pl.ANY)
+    return pl.pallas_call(
+        hold_kernel,
+        out_shape=jax.ShapeDtypeStruct(values.shape, values.dtype),
+        in_specs=[anywhere] * (1 + len(after)),
+        out_specs=anywhere,
+        input_output_aliases={0: 0},
+    )(values, *after)
 
 
 def ring_gather(values, send):
@@ -82,28 +105,24 @@
     return values[:rows] + send(values[rows:].astype(bf16)).astype(f32)
 
 
-def gather_rows(values):
-    values = ring_gather(values, lambda v, k: ring_send(v, "x", k))
-    values = jnp.concatenate([values, ring_send(values, "yh", 1)], axis=0)
-    values = ring_gather(values, lambda v, k: ring_send(v, "z", k))
-    return jnp.concatenate([values, ring_send(values, "core", 1)], axis=0)
-
-
-def reduce_rows(values):
-    values = pair_reduce(values, lambda v: ring_send(v, "core", 1))
-    values = ring_reduce(values, lambda v, k: ring_send(v, "z", k))
-    values = pair_reduce(values, lambda v: ring_send(v, "yh", 1))
-    return ring_reduce(values, lambda v, k: ring_send(v, "x", k))
+def z_send(values, shift):
+    return ring_send(values, "z", shift)
+
+
+def x_send(values, shift):
+    return ring_send(values, "x", shift)
+
+
+def both(values, send):
+    return jnp.concatenate([values, send(values)], axis=0)
 
 
 def gather_tokens(values):
-    values = ring_gather(values, y_send)
-    return jnp.concatenate([values, ring_send(values, "core", 1)], axis=0)
+    return both(ring_gather(values, y_send), core_send)
 
 
 def reduce_tokens(values):
-    values = pair_reduce(values, lambda v: ring_send(v, "core", 1))
-    return ring_reduce(values, y_send)
+    return ring_reduce(pair_reduce(values, core_send), y_send)
 
 
 def near(index):
@@ -223,6 +242,29 @@
     )(half, low, grad, logs, cos, sin)
 
 
+def cut_kernel(rank_ref, weight_ref, keep_ref, send_ref):
+    col = lax.broadcasted_iota(jnp.int32, (ROWS, FFT), 1)
+    for ref, i, flip in ((keep_ref, 0, 0), (keep_ref, 1, 6), (send_ref, 0, 1), (send_ref, 1, 7)):
+        rank = rank_ref[0] ^ flip
+        start = jnp.minimum(rank * FFT, FF - FFT)
+        inside = col >= rank * FFT - start
+        for k in range(3):
+            piece = weight_ref[:, pl.ds(pl.multiple_of(k * FF + start, 128), FFT)]
+            ref[i, :, k * FFT : (k + 1) * FFT] = jnp.where(inside, piece, 0.0).astype(bf16)
+
+
+def cut(rank, weight):
+    vmem = pl.BlockSpec(memory_space=pltpu.VMEM)
+    block = jax.ShapeDtypeStruct((2, ROWS, 3 * FFT), bf16)
+    return pl.pallas_call(
+        cut_kernel,
+        out_shape=(block, block),
+        in_specs=[pl.BlockSpec(memory_space=pltpu.SMEM), vmem],
+        out_specs=(vmem, vmem),
+        compiler_params=pltpu.CompilerParams(vmem_limit_bytes=32 * 1024 * 1024),
+    )(rank, weight)
+
+
 def adam_update(weight, moment_one, moment_two, gradient, step_rate):
     moment_one = 0.9 * moment_one + 0.1 * gradient
     moment_two = 0.95 * moment_two + 0.05 * gradient * gradient
@@ -251,48 +293,44 @@
     vector_moment_two,
 ):
     half = lax.axis_index("seq")
-    me = lax.axis_index("yh") * 2 + lax.axis_index("core")
+    yh, core = lax.axis_index("yh"), lax.axis_index("core")
+    side = half ^ yh
+    rank = half * 4 + yh * 2 + core
     halves = half.astype(jnp.int32).reshape(1)
     x_own, dy_own = inputs[0], cotangent[0]
-    x_all = jnp.concatenate([x_own, ring_send(x_own, "seq", 1)], axis=0)
+    ordered = lambda index, a, b: jnp.where(index == 0, jnp.stack([a, b]), jnp.stack([b, a]))
+
+    mlp_keep, mlp_give = cut(rank.astype(jnp.int32).reshape(1), mlp_weight)
+    mlp_got = core_send(mlp_give)
+    mlp_cores = ordered(core, mlp_keep, mlp_got)
+    mlp_block = ordered(yh, mlp_cores[:, 0], cross_send(mlp_cores[:, 1]))
+    mlp_w = lax.all_gather(mlp_block.reshape(4 * ROWS, 3 * FFT), ("z", "x"), axis=0, tiled=True)
+
+    x_all = both(x_own, seq_send)
 
     to_rel = one_hot(gathered_rows)
-    to_feat = one_hot(gathered_rows, half * HALF)
+    to_feat = one_hot(gathered_rows, side * HALF)
     to_mlp = one_hot(mlp_rows)
 
     attn_low = attn_weight.astype(bf16)
-    own_cols = lambda a, start, width: lax.dynamic_slice_in_dim(a, start + half * width, width, 1)
+    own_cols = lambda a, start, width: lax.dynamic_slice_in_dim(a, start + side * width, width, 1)
     vec_block = jnp.pad(vectors.astype(bf16)[None, :], ((0, ROWS - 1), (0, 48)))
-    proj_block = jnp.concatenate(
+    attn_block = jnp.concatenate(
         [
             own_cols(attn_low, 0, GROUP * HD),
             own_cols(attn_low, D, HD),
             own_cols(attn_low, D + KV * HD, HD),
             vec_block,
+            dot(attn_low[:, QKV:], to_mlp).astype(bf16),
         ],
         axis=1,
     )
-    out_block = dot(attn_low[:, QKV:], to_mlp).astype(bf16)
-    proj_all = gather_rows(proj_block)
-    out_w = gather_rows(out_block)
+    attn_x = ring_gather(attn_block, x_send)
+    proj_z = ring_gather(both(attn_x[:, : COLS + HD], cross_send), z_send)
+    proj_all = both(proj_z, core_send)
+    out_x = hold(attn_x[:, COLS + HD :], proj_z)
+    out_w = both(ring_gather(both(out_x, cross_send), z_send), core_send)
     proj_w = proj_all[:, :COLS]
-
-    mlp_low = jnp.pad(
-        mlp_weight.astype(bf16).reshape(ROWS, 3, FF), ((0, 0), (0, 0), (0, 8 * FFT - FF))
-    )
-    mlp_half = lax.dynamic_slice_in_dim(mlp_low, half * 4 * FFT, 4 * FFT, 2)
-    mlp_blocks = mlp_half.reshape(ROWS, 3, 4, FFT).transpose(2, 0, 1, 3).reshape(4, ROWS, 3 * FFT)
-    block = lambda a, i: lax.dynamic_index_in_dim(a, i, 0, keepdims=False)
-    mlp_rel = jnp.stack(
-        [
-            block(mlp_blocks, me),
-            ring_send(block(mlp_blocks, me ^ 1), "core", 1),
-            ring_send(block(mlp_blocks, me ^ 2), "yh", 1),
-            swap_both(block(mlp_blocks, me ^ 3)),
-        ]
-    )
-    mlp_rows_own = jnp.concatenate([block(mlp_rel, me ^ q) for q in range(4)], axis=0)
-    mlp_w = lax.all_gather(mlp_rows_own, ("z", "x"), axis=0, tiled=True)
 
     block_row = lax.broadcasted_iota(jnp.int32, (64, D), 0) * ROWS
     pick = (block_row == gathered_rows((64, D), 1)).astype(bf16)
@@ -312,14 +350,14 @@
     x_rel = dot(x_all, to_rel)
     x_mlp = dot(x_own, to_mlp)
     dy_low = dot(dy_own, to_mlp).astype(bf16)
-    dy_all = gather_tokens(dy_low)
+    dy_all = gather_tokens(hold(dy_low, proj_z))
     inv_one = lax.rsqrt(jnp.mean(x_rel * x_rel, axis=-1, keepdims=True) + norm_eps)
     unit_one = x_rel * inv_one
     normed = (unit_one * gain_one).astype(bf16)
     cos, sin = rotary_tables((jnp.arange(LEN) + half * TOK) % LEN)
     low, heads_out, logs = attend(halves, dot(normed, proj_w), bias, cos, sin)
     attended = jnp.concatenate(
-        [heads_out[:TOK], ring_send(heads_out[TOK:], "seq", 1)], axis=1
+        [heads_out[:TOK], seq_send(heads_out[TOK:])], axis=1
     )
     attended_rel = dot(attended, to_feat).astype(bf16)
     middle = x_mlp + dot(attended_rel, out_w)
@@ -336,13 +374,13 @@
     d_hidden = dot(dy_all, mlp_w[:, 2 * FFT :])
     d_gate = d_hidden * up * (sigmoid_gate * (1.0 + gate * (1.0 - sigmoid_gate)))
     d_gate_up = jnp.concatenate([d_gate, d_hidden * act], axis=1).astype(bf16)
-    d_second = reduce_tokens(dot_nt(d_gate_up, mlp_w[:, : 2 * FFT]))
-    down = reduce_tokens(dot_nt(hidden, mlp_w[:, 2 * FFT :]))
-    output = dot_nt((middle + down).astype(bf16), to_mlp).astype(bf16)[None]
     mlp_term = jnp.concatenate(
         [dot_tn(second_all, d_gate_up).astype(bf16), dot_tn(dy_all, hidden).astype(bf16)], axis=1
     )
     mlp_part = lax.psum_scatter(mlp_term, ("z", "x"), scatter_dimension=0, tiled=True)
+    d_second = reduce_tokens(dot_nt(hold(d_gate_up, mlp_term), mlp_w[:, : 2 * FFT]))
+    down = reduce_tokens(dot_nt(hold(hidden, d_second), mlp_w[:, 2 * FFT :]))
+    output = dot_nt((middle + down).astype(bf16), to_mlp).astype(bf16)[None]
 
     scaled_two = d_second * gain_two
     d_gain_two = jnp.sum(d_second * unit_two, axis=0, keepdims=True)
@@ -353,12 +391,12 @@
     d_branch = d_middle.astype(bf16)
     d_attended = dot_nt(dot_nt(d_branch, out_w).astype(bf16), to_feat).astype(bf16)
     d_heads = jnp.concatenate(
-        [d_attended[:, :HALF], ring_send(d_attended[:, HALF:], "seq", 1)], axis=0
+        [d_attended[:, :HALF], seq_send(d_attended[:, HALF:])], axis=0
     )
     d_proj, d_proj_sum = attend_back(halves, low, d_heads, logs, cos, sin)
     d_normed = dot_nt(d_proj, proj_w)
     d_gain_one = jnp.sum(d_normed * unit_one, axis=0, keepdims=True)
-    d_normed_own = d_normed[:TOK] + ring_send(d_normed[TOK:].astype(bf16), "seq", 1).astype(f32)
+    d_normed_own = d_normed[:TOK] + seq_send(d_normed[TOK:].astype(bf16)).astype(f32)
     scaled_one = d_normed_own * gain_one
     unit_own = unit_one[:TOK]
     through_norm = inv_one[:TOK] * (
@@ -367,7 +405,7 @@
     input_grad = split_dot(d_middle, to_mlp.T) + split_dot(through_norm, to_rel.T)
 
     bias_zero = jnp.zeros((1, QKV), f32)
-    put = lambda a, v, start, width: lax.dynamic_update_slice_in_dim(a, v, start + half * width, 1)
+    put = lambda a, v, start, width: lax.dynamic_update_slice_in_dim(a, v, start + side * width, 1)
     d_bias = put(bias_zero, d_proj_sum[:, : GROUP * HD], 0, GROUP * HD)
     d_bias = put(d_bias, d_proj_sum[:, GROUP * HD : (GROUP + 1) * HD], D, HD)
     d_bias = put(d_bias, d_proj_sum[:, (GROUP + 1) * HD :], D + KV * HD, HD)
@@ -375,17 +413,19 @@
         [split_dot(d_gain_one, to_rel.T), split_dot(d_gain_two, to_mlp.T), d_bias], axis=1
     )
     vec_term = jnp.pad(vec_term.reshape(64, 80).astype(bf16), ((0, 0), (0, 48)))
-    proj_part = reduce_rows(
-        jnp.concatenate([dot_tn(normed, d_proj), dot_tn(pick, vec_term)], axis=1)
-    )
-    out_part = reduce_rows(dot_tn(attended_rel, d_branch))
-
-    proj_low, out_low = proj_part.astype(bf16), out_part.astype(bf16)
-    proj_other = ring_send(proj_low, "seq", 1)
-    out_grad = out_low.astype(f32) + ring_send(out_low, "seq", 1).astype(f32)
-    vec_grad = (proj_low[:1, COLS : COLS + 80].astype(f32) + proj_other[:1, COLS : COLS + 80].astype(f32))[0]
-    first = jnp.where(half == 0, proj_low, proj_other).astype(f32)
-    last = jnp.where(half == 0, proj_other, proj_low).astype(f32)
+    out_term = pair_reduce(dot_tn(attended_rel, d_branch), core_send)
+    out_term = pair_reduce(ring_reduce(out_term, z_send), cross_send)
+    proj_term = jnp.concatenate([dot_tn(normed, d_proj), dot_tn(pick, vec_term)], axis=1)
+    proj_term = pair_reduce(proj_term, core_send)
+    proj_term = pair_reduce(ring_reduce(proj_term, z_send), cross_send)
+    attn_part = ring_reduce(jnp.concatenate([proj_term, out_term], axis=1), x_send).astype(bf16)
+
+    attn_other = seq_send(attn_part)
+    out_grad = attn_part[:, COLS + HD :].astype(f32) + attn_other[:, COLS + HD :].astype(f32)
+    vec_cols = slice(COLS, COLS + 80)
+    vec_grad = attn_part[0, vec_cols].astype(f32) + attn_other[0, vec_cols].astype(f32)
+    first = jnp.where(side == 0, attn_part, attn_other).astype(f32)
+    last = jnp.where(side == 0, attn_other, attn_part).astype(f32)
     query_end, key_end = GROUP * HD, (GROUP + 1) * HD
     attn_grad = jnp.concatenate(
         [
@@ -400,27 +440,18 @@
         axis=1,
     )
 
-    mlp_parts = mlp_part.reshape(4, ROWS, 3 * FFT)
-    grad_rel = jnp.stack(
-        [
-            block(mlp_parts, me),
-            ring_send(block(mlp_parts, me ^ 1), "core", 1),
-            ring_send(block(mlp_parts, me ^ 2), "yh", 1),
-            swap_both(block(mlp_parts, me ^ 3)),
-        ]
-    )
-    grad_half = jnp.stack([block(grad_rel, me ^ q) for q in range(4)])
-    grad_other = ring_send(grad_half, "seq", 1)
-    grad_all = jnp.concatenate(
-        [jnp.where(half == 0, grad_half, grad_other), jnp.where(half == 0, grad_other, grad_half)]
-    )
-    mlp_grad = (
-        grad_all.reshape(8, ROWS, 3, FFT)
-        .transpose(1, 2, 0, 3)
-        .reshape(ROWS, 3, 8 * FFT)[:, :, :FF]
-        .reshape(ROWS, 3 * FF)
-        .astype(f32)
-    )
+    by_core = mlp_part.reshape(2, 2, ROWS, 3 * FFT)
+    of_core = lambda c: lax.dynamic_index_in_dim(by_core, c, 1, keepdims=False)
+    pair = jnp.stack([of_core(core), core_send(of_core(1 - core))], axis=1)
+    near_rows = lax.dynamic_index_in_dim(pair, yh, 0, keepdims=False)
+    far_rows = lax.dynamic_index_in_dim(pair, 1 - yh, 0, keepdims=False)
+    by_flip = jnp.concatenate(
+        [near_rows, ring_send(far_rows, "yh", 1), seq_send(near_rows), cross_send(far_rows)]
+    )
+    by_rank = [lax.dynamic_index_in_dim(by_flip, rank ^ r, 0, keepdims=False) for r in range(8)]
+    by_rank = [p.reshape(ROWS, 3, FFT) for p in by_rank]
+    by_rank[7] = by_rank[7][:, :, 8 * FFT - FF :]
+    mlp_grad = jnp.concatenate(by_rank, axis=2).reshape(ROWS, 3 * FF).astype(f32)
 
     attn_one, attn_two, attn_new = adam_update(
         attn_weight, attn_moment_one, attn_moment_two, attn_grad, 0.05

time: 539 us -> 528 us (0.980)
  waiting for transfers between devices: 220 us -> 182 us
  local copies, waits for them, and re-layouts: 48.4 us -> 69.8 us
  starting transfers between devices: 81.7 us -> 63 us
  other arithmetic: 47.8 us -> 61 us
  matrix products: 111 us -> 120 us
    ppermute x47 -> x35, waiting for transfers between devices: 171 us -> 118 us  [ring_send(): lax.ppermute(values, axis, [(i, (i + shift) % size) for i in range(size)])]
    ppermute x47 -> x35, starting transfers between devices: 60.7 us -> 43.8 us  [ring_send(): lax.ppermute(values, axis, [(i, (i + shift) % size) for i in range(size)])]
    ppermute x2 -> x6, waiting for transfers between devices: 1.11 us -> 17.6 us  [cross_send(): return lax.ppermute(values, ('seq', 'yh'), [(i, 3 - i) for i in range(4)])]
    unnamed x224 -> x194, local copies, waits for them, and re-layouts: 28.7 us -> 42.3 us
    dot_general x22, matrix products: 60.1 us -> 67.9 us  [dot(): return jnp.dot(a, b, preferred_element_type=f32)]
    another operation x13 -> x9, other arithmetic: 11 us -> 11 us
  transfers between devices with their start and end apart: 63 -> 55, of which waited for: 34 -> 25; matrix products, arithmetic and copies ran while one was open for 25% -> 28% of each run, Pallas kernels for 1% -> 1%
where the time goes in v2:
time: 528 us; the launch traced here: 518 us
  waiting for transfers between devices  182 us (34%)
  matrix products  120 us (23%)
  local copies, waits for them, and re-layouts  69.8 us (13%)
  starting transfers between devices  63 us (12%)
  other arithmetic  61 us (12%)
  between operations  15.9 us (3%)
  Pallas kernels  5.66 us (1%)
    ppermute x35, waiting for transfers between devices, ring_send(): lax.ppermute(values, axis, [(i, (i + shift) % size) for i in range(size)])  118 us
    dot_general x22, matrix products, dot(): return jnp.dot(a, b, preferred_element_type=f32)  67.9 us
    ppermute x12, waiting for transfers between devices, y_send(): lax.ppermute(values, ('seq', 'yh'), [(place(i), place((i + shift) % 4)) f...  46.6 us
    ppermute x35, starting transfers between devices, ring_send(): lax.ppermute(values, axis, [(i, (i + shift) % size) for i in range(size)])  43.8 us
    unnamed x194, local copies, waits for them, and re-layouts  42.3 us
    dot_general x5, matrix products, dot_nt(): return lax.dot_general(a, b, contract_cols, preferred_element_type=f32)  31.9 us
    dot_general x5, matrix products, dot_tn(): return lax.dot_general(a, b, contract_rows, preferred_element_type=f32)  20.3 us
    ppermute x6, waiting for transfers between devices, cross_send(): return lax.ppermute(values, ('seq', 'yh'), [(i, 3 - i) for i in range(4)])  17.6 us
  transfers between devices with their start and end apart: 55, of which 25 were waited for; matrix products, arithmetic and copies ran while one was open for 28% of the time, Pallas kernels for 1%

profile of v2, /device:TPU:1, one launch (start us, length us, event | category | flops | bytes accessed | tf_op | source)
XLA Modules:
  0.0 517.9 jit_solution(14428934874578094972)
XLA Ops:
  22.8 5.2 %fusion.21 = pred[1536,1536]{1,0:T(32,128)(4,1)} fusion(s32[]{:T(128)S(6)} %mul.396, s32[1536]{0:T(1024)S(1)} %get-tuple-element.127, s32[1536]{0:T(1024)S(1)} %get-tuple-element.129, pred[1536]{0:T(1024)(128)(4,1)S(1)} %get-tuple-element.120, s32[1536]{0:T(1024)S(1)} %get-tuple-element.136, s32[1536]{0:T(1024)S(1)} %get-tuple-element.138, ...), kind=kLoop, calls=%fused_computation.64 | loop fusion | flops 268959744 | bytes 2428436 | tf_op jit(solution)/shard_map/eq | solution.py:279
  28.0 3.8 fusion.47
  37.0 4.0 convolution_bitcast_fusion
  41.0 3.8 collective-permute-done.20
  47.0 5.2 %fusion.20 = pred[1536,1536]{1,0:T(32,128)(4,1)} fusion(s32[1536]{0:T(1024)S(1)} %get-tuple-element.127, s32[1536]{0:T(1024)S(1)} %get-tuple-element.129, pred[1536]{0:T(1024)(128)(4,1)S(1)} %get-tuple-element.120, s32[1536]{0:T(1024)S(1)} %get-tuple-element.136, s32[1536]{0:T(1024)S(1)} %get-tuple-element.138, pred[1536]{0:T(1024)(128)(4,1)S(1)} %get-tuple-element.122, ...), kind=kLoop, calls=%fused_computation.63 | loop fusion | flops 266600448 | bytes 2428432 | tf_op jit(solution)/shard_map/eq | solution.py:279
  59.0 4.9 collective-permute-done.4
  71.5 11.4 %collective-permute-done.5 = bf16[192,1152]{1,0:T(8,128)(2,1)S(1)} collective-permute-done((bf16[192,1152]{1,0:T(8,128)(2,1)S(1)}, bf16[192,1152]{1,0:T(8,128)(2,1)S(1)}, u32[]{:S(2)}, u32[]{:S(2)}) %collective-permute-start.5) | collective-permute-done | bytes 442400 | tf_op jit(solution)/shard_map/ppermute | solution.py:54
  84.9 9.0 %collective-permute-done.7 = bf16[192,1152]{1,0:T(8,128)(2,1)S(1)} collective-permute-done((bf16[192,1152]{1,0:T(8,128)(2,1)S(1)}, bf16[192,1152]{1,0:T(8,128)(2,1)S(1)}, u32[]{:S(2)}, u32[]{:S(2)}) %collective-permute-start.7) | collective-permute-done | bytes 442400 | tf_op jit(solution)/shard_map/ppermute | solution.py:54
  97.5 3.5 multiply_reduce_fusion.1
  101.1 2.9 collective-permute-start.8
  111.8 22.1 %collective-permute-done.11 = bf16[192,1536]{1,0:T(8,128)(2,1)} collective-permute-done((bf16[192,1536]{1,0:T(8,128)(2,1)}, bf16[192,1536]{1,0:T(8,128)(2,1)}, u32[]{:S(2)}, u32[]{:S(2)}) %collective-permute-start.11) | collective-permute-done | bytes 589856 | tf_op jit(solution)/shard_map/ppermute | solution.py:54
  139.8 18.6 %collective-permute-done.13 = bf16[192,1536]{1,0:T(8,128)(2,1)S(1)} collective-permute-done((bf16[192,1536]{1,0:T(8,128)(2,1)}, bf16[192,1536]{1,0:T(8,128)(2,1)S(1)}, u32[]{:S(2)}, u32[]{:S(2)}) %collective-permute-start.13) | collective-permute-done | bytes 589856 | tf_op jit(solution)/shard_map/ppermute | solution.py:54
  159.5 3.0 collective-permute-start.14
  162.5 2.9 constant_dynamic-update-slice_fusion.9
  167.0 2.9 convolution_reduce_fusion.5
  169.9 3.5 fusion.42.qkv_ref
  179.0 3.4 collective-permute-done.9
  193.4 7.6 %collective-permute-done.15 = bf16[128,1536]{1,0:T(8,128)(2,1)S(1)} collective-permute-done((bf16[128,1536]{1,0:T(8,128)(2,1)S(1)}, bf16[128,1536]{1,0:T(8,128)(2,1)S(1)}, u32[]{:S(2)}, u32[]{:S(2)}) %collective-permute-start.15) | collective-permute-done | bytes 393248 | tf_op jit(solution)/shard_map/ppermute | solution.py:59
  201.0 8.6 %collective-permute-done.17 = bf16[128,1536]{1,0:T(8,128)(2,1)S(1)} collective-permute-done((bf16[128,1536]{1,0:T(8,128)(2,1)S(1)}, bf16[128,1536]{1,0:T(8,128)(2,1)S(1)}, u32[]{:S(2)}, u32[]{:S(2)}) %collective-permute-start.17) | collective-permute-done | bytes 393248 | tf_op jit(solution)/shard_map/ppermute | solution.py:59
  217.6 13.5 %fusion.30 = f32[1024,2304]{1,0:T(8,128)} fusion(bf16[1024,1536]{1,0:T(8,128)(2,1)} %constant_dynamic-update-slice_fusion.26, bf16[1536,3456]{1,0:T(8,128)(2,1)} %all-gather.2.cloned.1.call-done), kind=kOutput, calls=%fused_computation.77 | convolution fusion | flops 7247757312 | bytes 19660800 | tf_op jit(solution)/shard_map/dot_general | solution.py:35
  231.1 9.2 %multiply_convert_fusion.1 = (bf16[1024,1152]{1,0:T(8,128)(2,1)S(1)}, bf16[1024,1152]{1,0:T(8,128)(2,1)S(1)}, bf16[1024,1152]{1,0:T(8,128)(2,1)S(1)}) fusion(f32[1024,2304]{1,0:T(8,128)} %fusion.30, bf16[1024,1536]{1,0:T(8,128)(2,1)S(1)} %copy-done.55, bf16[1536,3456]{1,0:T(8,128)(2,1)} %all-gather.2.cloned.1.call-done), kind=kOutput, calls=%fused_computation.83 | convolution fusion | flops 3641573376 | bytes 23199744 | tf_op jit(solution)/shard_map/dot_general | solution.py:35
  240.3 11.0 %convolution_convert_fusion = bf16[1536,2304]{1,0:T(8,128)(2,1)S(1)} fusion(bf16[1024,1536]{1,0:T(8,128)(2,1)} %constant_dynamic-update-slice_fusion.26, bf16[1024,1152]{1,0:T(8,128)(2,1)S(1)} %get-tuple-element.54, bf16[1024,1152]{1,0:T(8,128)(2,1)S(1)} %get-tuple-element.53), kind=kOutput, calls=%fused_computation.41 | convolution fusion | flops 7260733440 | bytes 14942208 | tf_op jit(solution)/shard_map/dot_general | solution.py:39
  253.8 4.6 convolution_convert_fusion.1
  258.4 5.0 pad_maximum_fusion.refs_1_
  263.4 11.3 %fusion.28 = f32[1024,1536]{1,0:T(8,128)S(1)} fusion(bf16[1024,2304]{1,0:T(8,128)(2,1)} %shard_map.198, bf16[1536,3456]{1,0:T(8,128)(2,1)} %all-gather.2.cloned.1.call-done), kind=kOutput, calls=%fused_computation.75 | convolution fusion | flops 7247757312 | bytes 18087936 | tf_op jit(solution)/shard_map/dot_general | solution.py:43
  278.7 3.7 collective-permute-done.25
  282.4 4.5 fusion.153
  292.2 15.3 %collective-permute-done.26 = bf16[128,1536]{1,0:T(8,128)(2,1)} collective-permute-done((bf16[128,1536]{1,0:T(8,128)(2,1)}, bf16[128,1536]{1,0:T(8,128)(2,1)}, u32[]{:S(2)}, u32[]{:S(2)}) %collective-permute-start.26) | collective-permute-done | bytes 393248 | tf_op jit(solution)/shard_map/ppermute | solution.py:59
  307.4 3.2 collective-permute-done.27
  310.7 3.1 multiply_reduce_fusion.2
  315.7 7.3 %convolution_convert_fusion.2 = bf16[128,1536]{1,0:T(8,128)(2,1)} fusion(pred[1536,1536]{1,0:T(32,128)(4,1)} %fusion.21, bf16[128,1536]{1,0:T(8,128)(2,1)S(1)} %fusion.142, bf16[1536,1536]{1,0:T(8,128)(2,1)} %copy-done.21), kind=kOutput, calls=%fused_computation.113 | convolution fusion | flops 1208352768 | bytes 7864320 | tf_op jit(solution)/shard_map/dot_general | solution.py:43
  324.5 3.3 convolution_reduce_fusion
  330.6 3.5 copy-done.13
  342.3 4.2 multiply_reduce_fusion
  349.6 2.8 fusion.97
  356.8 6.5 %fusion.36 = f32[1024,1536]{1,0:T(8,128)S(1)} fusion(bf16[1024,1152]{1,0:T(8,128)(2,1)S(1)} %copy-done.33, bf16[1536,3456]{1,0:T(8,128)(2,1)} %all-gather.2.cloned.1.call-done), kind=kOutput, calls=%fused_computation.96 | convolution fusion | flops 3623878656 | bytes 12189696 | tf_op jit(solution)/shard_map/dot_general | solution.py:43
  382.1 4.3 collective-permute-done.36
  387.1 2.9 fusion.152
  390.0 7.0 %collective-permute-done.37 = bf16[192,1152]{1,0:T(8,128)(2,1)S(1)} collective-permute-done((bf16[192,1152]{1,0:T(8,128)(2,1)S(1)}, bf16[192,1152]{1,0:T(8,128)(2,1)S(1)}, u32[]{:S(2)}, u32[]{:S(2)}) %collective-permute-start.37) | collective-permute-done | bytes 442400 | tf_op jit(solution)/shard_map/ppermute | solution.py:54
  398.4 10.2 %collective-permute-done.41 = bf16[192,1536]{1,0:T(8,128)(2,1)S(1)} collective-permute-done((bf16[192,1536]{1,0:T(8,128)(2,1)S(1)}, bf16[192,1536]{1,0:T(8,128)(2,1)S(1)}, u32[]{:S(2)}, u32[]{:S(2)}) %collective-permute-start.41) | collective-permute-done | bytes 589856 | tf_op jit(solution)/shard_map/ppermute | solution.py:54
  408.5 14.4 %collective-permute-done.42 = bf16[192,1536]{1,0:T(8,128)(2,1)S(1)} collective-permute-done((bf16[192,1536]{1,0:T(8,128)(2,1)S(1)}, bf16[192,1536]{1,0:T(8,128)(2,1)S(1)}, u32[]{:S(2)}, u32[]{:S(2)}) %collective-permute-start.42) | collective-permute-done | bytes 589856 | tf_op jit(solution)/shard_map/ppermute | solution.py:54
  423.8 7.7 %collective-permute-done.44 = bf16[96,1536]{1,0:T(8,128)(2,1)S(1)} collective-permute-done((bf16[96,1536]{1,0:T(8,128)(2,1)S(1)}, bf16[96,1536]{1,0:T(8,128)(2,1)S(1)}, u32[]{:S(2)}, u32[]{:S(2)}) %collective-permute-start.44) | collective-permute-done | bytes 294944 | tf_op jit(solution)/shard_map/ppermute | solution.py:65
  443.0 8.0 %collective-permute-done.32 = bf16[128,1536]{1,0:T(8,128)(2,1)S(1)} collective-permute-done((bf16[128,1536]{1,0:T(8,128)(2,1)S(1)}, bf16[128,1536]{1,0:T(8,128)(2,1)S(1)}, u32[]{:S(2)}, u32[]{:S(2)}) %collective-permute-start.32) | collective-permute-done | bytes 393248 | tf_op jit(solution)/shard_map/ppermute | solution.py:59
  457.6 5.5 %collective-permute-start.49 = (bf16[2,24,3456]{2,1,0:T(8,128)(2,1)S(1)}, bf16[2,24,3456]{2,1,0:T(8,128)(2,1)S(1)}, u32[]{:S(2)}, u32[]{:S(2)}) collective-permute-start(bf16[2,24,3456]{2,1,0:T(8,128)(2,1)S(1)} %get-tuple-element.78), channel_id=1, source_target_pairs={{0,1},{1,0},{2,3},{3,2},{4,5},{5,4},{6,7},{7,6},{8,9},{9,8},{10,11... | collective-permute-start | bytes 995336 | tf_op jit(solution)/shard_map/ppermute | solution.py:54
  464.4 3.7 fusion.49
  473.8 5.5 %collective-permute-done.50 = bf16[2,24,3456]{2,1,0:T(8,128)(2,1)S(1)} collective-permute-done((bf16[2,24,3456]{2,1,0:T(8,128)(2,1)S(1)}, bf16[2,24,3456]{2,1,0:T(8,128)(2,1)S(1)}, u32[]{:S(2)}, u32[]{:S(2)}) %collective-permute-start.50) | collective-permute-done | bytes 331808 | tf_op jit(solution)/shard_map/ppermute | solution.py:54
  479.3 6.2 %collective-permute-done.51 = bf16[2,24,3456]{2,1,0:T(8,128)(2,1)S(1)} collective-permute-done((bf16[2,24,3456]{2,1,0:T(8,128)(2,1)S(1)}, bf16[2,24,3456]{2,1,0:T(8,128)(2,1)S(1)}, u32[]{:S(2)}, u32[]{:S(2)}) %collective-permute-start.51) | collective-permute-done | bytes 331808 | tf_op jit(solution)/shard_map/ppermute | solution.py:54
  506.2 4.6 multiply_subtract_fusion
  (411 shorter events, 183.8 us)
Async XLA Ops:
  7.2 210.4 %all-gather.2.cloned.1.call-start = ((), (), s32[]{:S(2)}) async-start(), calls=%async_computation.1 | async-start | bytes 11280384 | tf_op jit(solution)/shard_map/all_gather | solution.py:307
  13.7 41.1 %collective-permute-start.1 = (bf16[24,2688]{1,0:T(8,128)(2,1)S(1)}, bf16[24,2688]{1,0:T(8,128)(2,1)}, u32[]{:S(2)}, u32[]{:S(2)}) collective-permute-start(bf16[24,2688]{1,0:T(8,128)(2,1)S(1)} %fusion.51), channel_id=1, source_target_pairs={{0,2},{2,4},{4,6},{6,0},{1,3},{3,5},{5,7},{7,1},{8,10},{10,12},{12... | collective-permute-start | bytes 387080 | tf_op jit(solution)/shard_map/ppermute | solution.py:54
  15.8 39.0 %collective-permute-start.2 = (bf16[24,2688]{1,0:T(8,128)(2,1)S(1)}, bf16[24,2688]{1,0:T(8,128)(2,1)}, u32[]{:S(2)}, u32[]{:S(2)}) collective-permute-start(bf16[24,2688]{1,0:T(8,128)(2,1)S(1)} %fusion.51), channel_id=1, source_target_pairs={{0,6},{2,0},{4,2},{6,4},{1,7},{3,1},{5,3},{7,5},{8,14},{10,8},{12,... | collective-permute-start | bytes 387080 | tf_op jit(solution)/shard_map/ppermute | solution.py:54
  17.1 37.7 %collective-permute-start.3 = (bf16[24,2688]{1,0:T(8,128)(2,1)S(1)}, bf16[24,2688]{1,0:T(8,128)(2,1)}, u32[]{:S(2)}, u32[]{:S(2)}) collective-permute-start(bf16[24,2688]{1,0:T(8,128)(2,1)S(1)} %fusion.51), channel_id=1, source_target_pairs={{0,4},{2,6},{4,0},{6,2},{1,5},{3,7},{5,1},{7,3},{8,12},{10,14},{12... | collective-permute-start | bytes 387080 | tf_op jit(solution)/shard_map/ppermute | solution.py:54
  18.8 78.7 %collective-permute-start = (bf16[128,1536]{1,0:T(8,128)(2,1)}, bf16[128,1536]{1,0:T(8,128)(2,1)}, u32[]{:S(2)}, u32[]{:S(2)}) collective-permute-start(bf16[128,1536]{1,0:T(8,128)(2,1)} %bitcast), channel_id=1, source_target_pairs={{0,64},{64,0},{1,65},{65,1},{2,66},{66,2},{3,67},{67,3},{4,68},{68... | collective-permute-start | bytes 1179656 | tf_op jit(solution)/shard_map/ppermute | solution.py:54
  20.9 11.0 %collective-permute-start.19 = (bf16[2,24,3456]{2,1,0:T(8,128)(2,1)}, bf16[2,24,3456]{2,1,0:T(8,128)(2,1)}, u32[]{:S(2)}, u32[]{:S(2)}) collective-permute-start(bf16[2,24,3456]{2,1,0:T(8,128)(2,1)} %get-tuple-element.20), channel_id=1, source_target_pairs={{0,1},{1,0},{2,3},{3,2},{4,5},{5,4},{6,7},{7,6},{8,9},{9,8},{10,11... | collective-permute-start | bytes 995336 | tf_op jit(solution)/shard_map/ppermute | solution.py:54
  33.8 10.9 %collective-permute-start.20 = (bf16[2,24,3456]{2,1,0:T(8,128)(2,1)}, bf16[2,24,3456]{2,1,0:T(8,128)(2,1)}, u32[]{:S(2)}, u32[]{:S(2)}) collective-permute-start(bf16[2,24,3456]{2,1,0:T(8,128)(2,1)} %get-tuple-element.81), channel_id=1, source_target_pairs={{0,72},{8,64},{64,8},{72,0},{1,73},{9,65},{65,9},{73,1},{2,74},{10... | collective-permute-start | bytes 995336 | tf_op jit(solution)/shard_map/ppermute | solution.py:65
  46.9 409.4 %reduce-scatter.2.cloned.1.call-start = ((), (), s32[]{:S(2)}) async-start(), calls=%async_computation.2 | async-start | bytes 11280384 | tf_op jit(solution)/shard_map/reduce_scatter | solution.py:380
  56.4 7.5 %collective-permute-start.4 = (bf16[96,1152]{1,0:T(8,128)(2,1)S(1)}, bf16[96,1152]{1,0:T(8,128)(2,1)S(1)}, u32[]{:S(2)}, u32[]{:S(2)}) collective-permute-start(bf16[96,1152]{1,0:T(8,128)(2,1)S(1)} %get-tuple-element.52), channel_id=1, source_target_pairs={{0,72},{8,64},{64,8},{72,0},{1,73},{9,65},{65,9},{73,1},{2,74},{10... | collective-permute-start | bytes 663560 | tf_op jit(solution)/shard_map/ppermute | solution.py:65
  63.9 19.0 %collective-permute-start.5 = (bf16[192,1152]{1,0:T(8,128)(2,1)S(1)}, bf16[192,1152]{1,0:T(8,128)(2,1)S(1)}, u32[]{:S(2)}, u32[]{:S(2)}) collective-permute-start(bf16[192,1152]{1,0:T(8,128)(2,1)S(1)} %pad_maximum_fusion.8), channel_id=1, source_target_pairs={{0,16},{16,32},{32,48},{48,0},{1,17},{17,33},{33,49},{49,1},{2,18}... | collective-permute-start | bytes 1327112 | tf_op jit(solution)/shard_map/ppermute | solution.py:54
  67.3 16.6 %collective-permute-start.6 = (bf16[192,1152]{1,0:T(8,128)(2,1)S(1)}, bf16[192,1152]{1,0:T(8,128)(2,1)S(1)}, u32[]{:S(2)}, u32[]{:S(2)}) collective-permute-start(bf16[192,1152]{1,0:T(8,128)(2,1)S(1)} %pad_maximum_fusion.8), channel_id=1, source_target_pairs={{0,48},{16,0},{32,16},{48,32},{1,49},{17,1},{33,17},{49,33},{2,50}... | collective-permute-start | bytes 1327112 | tf_op jit(solution)/shard_map/ppermute | solution.py:54
  69.4 24.5 %collective-permute-start.7 = (bf16[192,1152]{1,0:T(8,128)(2,1)S(1)}, bf16[192,1152]{1,0:T(8,128)(2,1)S(1)}, u32[]{:S(2)}, u32[]{:S(2)}) collective-permute-start(bf16[192,1152]{1,0:T(8,128)(2,1)S(1)} %pad_maximum_fusion.8), channel_id=1, source_target_pairs={{0,32},{16,48},{32,0},{48,16},{1,33},{17,49},{33,1},{49,17},{2,34}... | collective-permute-start | bytes 1327112 | tf_op jit(solution)/shard_map/ppermute | solution.py:54
  95.0 8.9 %collective-permute-start.10 = (bf16[96,1536]{1,0:T(8,128)(2,1)}, bf16[96,1536]{1,0:T(8,128)(2,1)S(1)}, u32[]{:S(2)}, u32[]{:S(2)}) collective-permute-start(bf16[96,1536]{1,0:T(8,128)(2,1)} %shard_map.195), channel_id=1, source_target_pairs={{0,72},{8,64},{64,8},{72,0},{1,73},{9,65},{65,9},{73,1},{2,74},{10... | collective-permute-start | bytes 884744 | tf_op jit(solution)/shard_map/ppermute | solution.py:65
  101.1 61.5 %collective-permute-start.8 = (bf16[768,1152]{1,0:T(8,128)(2,1)}, bf16[768,1152]{1,0:T(8,128)(2,1)}, u32[]{:S(2)}, u32[]{:S(2)}) collective-permute-start(bf16[768,1152]{1,0:T(8,128)(2,1)} %get-tuple-element.91.refs_1_), channel_id=1, source_target_pairs={{0,1},{1,0},{2,3},{3,2},{4,5},{5,4},{6,7},{7,6},{8,9},{9,8},{10,11... | collective-permute-start | bytes 5308424 | tf_op jit(solution)/shard_map/ppermute | solution.py:54
  104.8 29.0 %collective-permute-start.11 = (bf16[192,1536]{1,0:T(8,128)(2,1)}, bf16[192,1536]{1,0:T(8,128)(2,1)}, u32[]{:S(2)}, u32[]{:S(2)}) collective-permute-start(bf16[192,1536]{1,0:T(8,128)(2,1)} %pad_maximum_fusion.7), channel_id=1, source_target_pairs={{0,16},{16,32},{32,48},{48,0},{1,17},{17,33},{33,49},{49,1},{2,18}... | collective-permute-start | bytes 1769480 | tf_op jit(solution)/shard_map/ppermute | solution.py:54
  106.9 29.8 %collective-permute-start.12 = (bf16[192,1536]{1,0:T(8,128)(2,1)}, bf16[192,1536]{1,0:T(8,128)(2,1)}, u32[]{:S(2)}, u32[]{:S(2)}) collective-permute-start(bf16[192,1536]{1,0:T(8,128)(2,1)} %pad_maximum_fusion.7), channel_id=1, source_target_pairs={{0,48},{16,0},{32,16},{48,32},{1,49},{17,1},{33,17},{49,33},{2,50}... | collective-permute-start | bytes 1769480 | tf_op jit(solution)/shard_map/ppermute | solution.py:54
  109.9 65.9 %collective-permute-start.21 = (bf16[128,1536]{1,0:T(8,128)(2,1)}, bf16[128,1536]{1,0:T(8,128)(2,1)S(1)}, u32[]{:S(2)}, u32[]{:S(2)}) collective-permute-start(bf16[128,1536]{1,0:T(8,128)(2,1)} %shard_map.197), channel_id=1, source_target_pairs={{0,64},{64,8},{8,72},{72,0},{1,65},{65,9},{9,73},{73,1},{2,66},{66... | collective-permute-start | bytes 1179656 | tf_op jit(solution)/shard_map/ppermute | solution.py:59
  109.9 48.5 %collective-permute-start.13 = (bf16[192,1536]{1,0:T(8,128)(2,1)}, bf16[192,1536]{1,0:T(8,128)(2,1)S(1)}, u32[]{:S(2)}, u32[]{:S(2)}) collective-permute-start(bf16[192,1536]{1,0:T(8,128)(2,1)} %pad_maximum_fusion.7), channel_id=1, source_target_pairs={{0,32},{16,48},{32,0},{48,16},{1,33},{17,49},{33,1},{49,17},{2,34}... | collective-permute-start | bytes 1769480 | tf_op jit(solution)/shard_map/ppermute | solution.py:54
  133.9 41.9 %collective-permute-start.22 = (bf16[128,1536]{1,0:T(8,128)(2,1)}, bf16[128,1536]{1,0:T(8,128)(2,1)}, u32[]{:S(2)}, u32[]{:S(2)}) collective-permute-start(bf16[128,1536]{1,0:T(8,128)(2,1)} %shard_map.197), channel_id=1, source_target_pairs={{0,72},{64,0},{8,64},{72,8},{1,73},{65,1},{9,65},{73,9},{2,74},{66... | collective-permute-start | bytes 1179656 | tf_op jit(solution)/shard_map/ppermute | solution.py:59
  136.7 39.1 %collective-permute-start.23 = (bf16[128,1536]{1,0:T(8,128)(2,1)}, bf16[128,1536]{1,0:T(8,128)(2,1)}, u32[]{:S(2)}, u32[]{:S(2)}) collective-permute-start(bf16[128,1536]{1,0:T(8,128)(2,1)} %shard_map.197), channel_id=1, source_target_pairs={{0,8},{64,72},{8,0},{72,64},{1,9},{65,73},{9,1},{73,65},{2,10},{66... | collective-permute-start | bytes 1179656 | tf_op jit(solution)/shard_map/ppermute | solution.py:59
  159.5 24.4 %collective-permute-start.14 = (bf16[768,1536]{1,0:T(8,128)(2,1)}, bf16[768,1536]{1,0:T(8,128)(2,1)}, u32[]{:S(2)}, u32[]{:S(2)}) collective-permute-start(bf16[768,1536]{1,0:T(8,128)(2,1)} %get-tuple-element.82), channel_id=1, source_target_pairs={{0,1},{1,0},{2,3},{3,2},{4,5},{5,4},{6,7},{7,6},{8,9},{9,8},{10,11... | collective-permute-start | bytes 7077896 | tf_op jit(solution)/shard_map/ppermute | solution.py:54
  177.6 35.9 %collective-permute-start.24 = (bf16[512,1536]{1,0:T(8,128)(2,1)S(1)}, bf16[512,1536]{1,0:T(8,128)(2,1)S(1)}, u32[]{:S(2)}, u32[]{:S(2)}) collective-permute-start(bf16[512,1536]{1,0:T(8,128)(2,1)S(1)} %pad_maximum_fusion.4), channel_id=1, source_target_pairs={{0,1},{1,0},{2,3},{3,2},{4,5},{5,4},{6,7},{7,6},{8,9},{9,8},{10,11... | collective-permute-start | bytes 4718600 | tf_op jit(solution)/shard_map/ppermute | solution.py:54
  189.9 11.1 %collective-permute-start.15 = (bf16[128,1536]{1,0:T(8,128)(2,1)S(1)}, bf16[128,1536]{1,0:T(8,128)(2,1)S(1)}, u32[]{:S(2)}, u32[]{:S(2)}) collective-permute-start(bf16[128,1536]{1,0:T(8,128)(2,1)S(1)} %get-tuple-element.50), channel_id=1, source_target_pairs={{0,64},{64,8},{8,72},{72,0},{1,65},{65,9},{9,73},{73,1},{2,66},{66... | collective-permute-start | bytes 1179656 | tf_op jit(solution)/shard_map/ppermute | solution.py:59
  190.1 10.9 %collective-permute-start.16 = (bf16[128,1536]{1,0:T(8,128)(2,1)S(1)}, bf16[128,1536]{1,0:T(8,128)(2,1)S(1)}, u32[]{:S(2)}, u32[]{:S(2)}) collective-permute-start(bf16[128,1536]{1,0:T(8,128)(2,1)S(1)} %get-tuple-element.50), channel_id=1, source_target_pairs={{0,72},{64,0},{8,64},{72,8},{1,73},{65,1},{9,65},{73,9},{2,74},{66... | collective-permute-start | bytes 1179656 | tf_op jit(solution)/shard_map/ppermute | solution.py:59
  192.6 17.0 %collective-permute-start.17 = (bf16[128,1536]{1,0:T(8,128)(2,1)S(1)}, bf16[128,1536]{1,0:T(8,128)(2,1)S(1)}, u32[]{:S(2)}, u32[]{:S(2)}) collective-permute-start(bf16[128,1536]{1,0:T(8,128)(2,1)S(1)} %get-tuple-element.50), channel_id=1, source_target_pairs={{0,8},{64,72},{8,0},{72,64},{1,9},{65,73},{9,1},{73,65},{2,10},{66... | collective-permute-start | bytes 1179656 | tf_op jit(solution)/shard_map/ppermute | solution.py:59
  288.0 19.5 %collective-permute-start.26 = (bf16[128,1536]{1,0:T(8,128)(2,1)}, bf16[128,1536]{1,0:T(8,128)(2,1)}, u32[]{:S(2)}, u32[]{:S(2)}) collective-permute-start(bf16[128,1536]{1,0:T(8,128)(2,1)} %get-tuple-element.65), channel_id=1, source_target_pairs={{0,72},{64,0},{8,64},{72,8},{1,73},{65,1},{9,65},{73,9},{2,74},{66... | collective-permute-start | bytes 1179656 | tf_op jit(solution)/shard_map/ppermute | solution.py:59
  290.5 20.2 %collective-permute-start.27 = (bf16[128,1536]{1,0:T(8,128)(2,1)}, bf16[128,1536]{1,0:T(8,128)(2,1)}, u32[]{:S(2)}, u32[]{:S(2)}) collective-permute-start(bf16[128,1536]{1,0:T(8,128)(2,1)} %get-tuple-element.67), channel_id=1, source_target_pairs={{0,64},{64,8},{8,72},{72,0},{1,65},{65,9},{9,73},{73,1},{2,66},{66... | collective-permute-start | bytes 1179656 | tf_op jit(solution)/shard_map/ppermute | solution.py:59
  290.5 20.2 %collective-permute-start.28 = (bf16[128,1536]{1,0:T(8,128)(2,1)S(1)}, bf16[128,1536]{1,0:T(8,128)(2,1)}, u32[]{:S(2)}, u32[]{:S(2)}) collective-permute-start(bf16[128,1536]{1,0:T(8,128)(2,1)S(1)} %get-tuple-element.66), channel_id=1, source_target_pairs={{0,8},{64,72},{8,0},{72,64},{1,9},{65,73},{9,1},{73,65},{2,10},{66... | collective-permute-start | bytes 1179656 | tf_op jit(solution)/shard_map/ppermute | solution.py:59
  324.3 15.2 %collective-permute-start.33 = (bf16[128,768]{1,0:T(8,128)(2,1)S(1)}, bf16[128,768]{1,0:T(8,128)(2,1)S(1)}, u32[]{:S(2)}, u32[]{:S(2)}) collective-permute-start(bf16[128,768]{1,0:T(8,128)(2,1)S(1)} %get-tuple-element.98), channel_id=1, source_target_pairs={{0,64},{64,0},{1,65},{65,1},{2,66},{66,2},{3,67},{67,3},{4,68},{68... | collective-permute-start | bytes 589832 | tf_op jit(solution)/shard_map/ppermute | solution.py:54
  335.8 41.3 %collective-permute-start.40 = (bf16[768,1536]{1,0:T(8,128)(2,1)}, bf16[768,1536]{1,0:T(8,128)(2,1)}, u32[]{:S(2)}, u32[]{:S(2)}) collective-permute-start(bf16[768,1536]{1,0:T(8,128)(2,1)} %slice.517), channel_id=1, source_target_pairs={{0,1},{1,0},{2,3},{3,2},{4,5},{5,4},{6,7},{7,6},{8,9},{9,8},{10,11... | collective-permute-start | bytes 7077896 | tf_op jit(solution)/shard_map/ppermute | solution.py:54
  353.2 20.9 %collective-permute-start.35 = (bf16[768,1152]{1,0:T(8,128)(2,1)S(1)}, bf16[768,1152]{1,0:T(8,128)(2,1)S(1)}, u32[]{:S(2)}, u32[]{:S(2)}) collective-permute-start(bf16[768,1152]{1,0:T(8,128)(2,1)S(1)} %fusion.35), channel_id=1, source_target_pairs={{0,1},{1,0},{2,3},{3,2},{4,5},{5,4},{6,7},{7,6},{8,9},{9,8},{10,11... | collective-permute-start | bytes 5308424 | tf_op jit(solution)/shard_map/ppermute | solution.py:54
  354.4 14.9 %collective-permute-start.34 = (bf16[128,1536]{1,0:T(8,128)(2,1)S(1)}, bf16[128,1536]{1,0:T(8,128)(2,1)S(1)}, u32[]{:S(2)}, u32[]{:S(2)}) collective-permute-start(bf16[128,1536]{1,0:T(8,128)(2,1)S(1)} %slice.520), channel_id=1, source_target_pairs={{0,64},{64,0},{1,65},{65,1},{2,66},{66,2},{3,67},{67,3},{4,68},{68... | collective-permute-start | bytes 1179656 | tf_op jit(solution)/shard_map/ppermute | solution.py:54
  364.6 17.1 %collective-permute-start.29 = (bf16[512,1536]{1,0:T(8,128)(2,1)}, bf16[512,1536]{1,0:T(8,128)(2,1)}, u32[]{:S(2)}, u32[]{:S(2)}) collective-permute-start(bf16[512,1536]{1,0:T(8,128)(2,1)} %slice.518), channel_id=1, source_target_pairs={{0,1},{1,0},{2,3},{3,2},{4,5},{5,4},{6,7},{7,6},{8,9},{9,8},{10,11... | collective-permute-start | bytes 4718600 | tf_op jit(solution)/shard_map/ppermute | solution.py:54
  374.9 11.5 %collective-permute-start.36 = (bf16[192,1152]{1,0:T(8,128)(2,1)S(1)}, bf16[192,1152]{1,0:T(8,128)(2,1)S(1)}, u32[]{:S(2)}, u32[]{:S(2)}) collective-permute-start(bf16[192,1152]{1,0:T(8,128)(2,1)S(1)} %get-tuple-element.59), channel_id=1, source_target_pairs={{0,48},{16,0},{32,16},{48,32},{1,49},{17,1},{33,17},{49,33},{2,50}... | collective-permute-start | bytes 1327112 | tf_op jit(solution)/shard_map/ppermute | solution.py:54
  375.9 21.2 %collective-permute-start.37 = (bf16[192,1152]{1,0:T(8,128)(2,1)S(1)}, bf16[192,1152]{1,0:T(8,128)(2,1)S(1)}, u32[]{:S(2)}, u32[]{:S(2)}) collective-permute-start(bf16[192,1152]{1,0:T(8,128)(2,1)S(1)} %get-tuple-element.61), channel_id=1, source_target_pairs={{0,16},{16,32},{32,48},{48,0},{1,17},{17,33},{33,49},{49,1},{2,18}... | collective-permute-start | bytes 1327112 | tf_op jit(solution)/shard_map/ppermute | solution.py:54
  376.4 20.6 %collective-permute-start.38 = (bf16[192,1152]{1,0:T(8,128)(2,1)S(1)}, bf16[192,1152]{1,0:T(8,128)(2,1)S(1)}, u32[]{:S(2)}, u32[]{:S(2)}) collective-permute-start(bf16[192,1152]{1,0:T(8,128)(2,1)S(1)} %get-tuple-element.60), channel_id=1, source_target_pairs={{0,32},{16,48},{32,0},{48,16},{1,33},{17,49},{33,1},{49,17},{2,34}... | collective-permute-start | bytes 1327112 | tf_op jit(solution)/shard_map/ppermute | solution.py:54
  379.9 28.6 %collective-permute-start.41 = (bf16[192,1536]{1,0:T(8,128)(2,1)S(1)}, bf16[192,1536]{1,0:T(8,128)(2,1)S(1)}, u32[]{:S(2)}, u32[]{:S(2)}) collective-permute-start(bf16[192,1536]{1,0:T(8,128)(2,1)S(1)} %get-tuple-element.56), channel_id=1, source_target_pairs={{0,48},{16,0},{32,16},{48,32},{1,49},{17,1},{33,17},{49,33},{2,50}... | collective-permute-start | bytes 1769480 | tf_op jit(solution)/shard_map/ppermute | solution.py:54
  381.8 41.2 %collective-permute-start.42 = (bf16[192,1536]{1,0:T(8,128)(2,1)S(1)}, bf16[192,1536]{1,0:T(8,128)(2,1)S(1)}, u32[]{:S(2)}, u32[]{:S(2)}) collective-permute-start(bf16[192,1536]{1,0:T(8,128)(2,1)S(1)} %get-tuple-element.58), channel_id=1, source_target_pairs={{0,16},{16,32},{32,48},{48,0},{1,17},{17,33},{33,49},{49,1},{2,18}... | collective-permute-start | bytes 1769480 | tf_op jit(solution)/shard_map/ppermute | solution.py:54
  386.4 36.6 %collective-permute-start.43 = (bf16[192,1536]{1,0:T(8,128)(2,1)S(1)}, bf16[192,1536]{1,0:T(8,128)(2,1)S(1)}, u32[]{:S(2)}, u32[]{:S(2)}) collective-permute-start(bf16[192,1536]{1,0:T(8,128)(2,1)S(1)} %get-tuple-element.57), channel_id=1, source_target_pairs={{0,32},{16,48},{32,0},{48,16},{1,33},{17,49},{33,1},{49,17},{2,34}... | collective-permute-start | bytes 1769480 | tf_op jit(solution)/shard_map/ppermute | solution.py:54
  397.2 26.5 %collective-permute-start.39 = (bf16[96,1152]{1,0:T(8,128)(2,1)S(1)}, bf16[96,1152]{1,0:T(8,128)(2,1)S(1)}, u32[]{:S(2)}, u32[]{:S(2)}) collective-permute-start(bf16[96,1152]{1,0:T(8,128)(2,1)S(1)} %slice.522), channel_id=1, source_target_pairs={{0,72},{8,64},{64,8},{72,0},{1,73},{9,65},{65,9},{73,1},{2,74},{10... | collective-permute-start | bytes 663560 | tf_op jit(solution)/shard_map/ppermute | solution.py:65
  423.2 8.3 %collective-permute-start.44 = (bf16[96,1536]{1,0:T(8,128)(2,1)S(1)}, bf16[96,1536]{1,0:T(8,128)(2,1)S(1)}, u32[]{:S(2)}, u32[]{:S(2)}) collective-permute-start(bf16[96,1536]{1,0:T(8,128)(2,1)S(1)} %slice.521), channel_id=1, source_target_pairs={{0,72},{8,64},{64,8},{72,0},{1,73},{9,65},{65,9},{73,1},{2,74},{10... | collective-permute-start | bytes 884744 | tf_op jit(solution)/shard_map/ppermute | solution.py:65
  434.6 8.4 %collective-permute-start.31 = (bf16[128,1536]{1,0:T(8,128)(2,1)S(1)}, bf16[128,1536]{1,0:T(8,128)(2,1)S(1)}, u32[]{:S(2)}, u32[]{:S(2)}) collective-permute-start(bf16[128,1536]{1,0:T(8,128)(2,1)S(1)} %get-tuple-element.64), channel_id=1, source_target_pairs={{0,64},{64,8},{8,72},{72,0},{1,65},{65,9},{9,73},{73,1},{2,66},{66... | collective-permute-start | bytes 1179656 | tf_op jit(solution)/shard_map/ppermute | solution.py:59
  435.6 15.4 %collective-permute-start.32 = (bf16[128,1536]{1,0:T(8,128)(2,1)S(1)}, bf16[128,1536]{1,0:T(8,128)(2,1)S(1)}, u32[]{:S(2)}, u32[]{:S(2)}) collective-permute-start(bf16[128,1536]{1,0:T(8,128)(2,1)S(1)} %get-tuple-element.63), channel_id=1, source_target_pairs={{0,8},{64,72},{8,0},{72,64},{1,9},{65,73},{9,1},{73,65},{2,10},{66... | collective-permute-start | bytes 1179656 | tf_op jit(solution)/shard_map/ppermute | solution.py:59
  439.0 14.6 %collective-permute-start.48 = (bf16[24,2688]{1,0:T(8,128)(2,1)S(1)}, bf16[24,2688]{1,0:T(8,128)(2,1)S(1)}, u32[]{:S(2)}, u32[]{:S(2)}) collective-permute-start(bf16[24,2688]{1,0:T(8,128)(2,1)S(1)} %fusion.102), channel_id=1, source_target_pairs={{0,64},{64,0},{1,65},{65,1},{2,66},{66,2},{3,67},{67,3},{4,68},{68... | collective-permute-start | bytes 387080 | tf_op jit(solution)/shard_map/ppermute | solution.py:54
  457.6 10.5 %collective-permute-start.49 = (bf16[2,24,3456]{2,1,0:T(8,128)(2,1)S(1)}, bf16[2,24,3456]{2,1,0:T(8,128)(2,1)S(1)}, u32[]{:S(2)}, u32[]{:S(2)}) collective-permute-start(bf16[2,24,3456]{2,1,0:T(8,128)(2,1)S(1)} %get-tuple-element.78), channel_id=1, source_target_pairs={{0,1},{1,0},{2,3},{3,2},{4,5},{5,4},{6,7},{7,6},{8,9},{9,8},{10,11... | collective-permute-start | bytes 995336 | tf_op jit(solution)/shard_map/ppermute | solution.py:54
  468.3 11.0 %collective-permute-start.50 = (bf16[2,24,3456]{2,1,0:T(8,128)(2,1)S(1)}, bf16[2,24,3456]{2,1,0:T(8,128)(2,1)S(1)}, u32[]{:S(2)}, u32[]{:S(2)}) collective-permute-start(bf16[2,24,3456]{2,1,0:T(8,128)(2,1)S(1)} %get-tuple-element.77), channel_id=1, source_target_pairs={{0,8},{8,0},{1,9},{9,1},{2,10},{10,2},{3,11},{11,3},{4,12},{12,4},... | collective-permute-start | bytes 995336 | tf_op jit(solution)/shard_map/ppermute | solution.py:54
  470.4 16.3 %collective-permute-start.52 = (bf16[2,24,3456]{2,1,0:T(8,128)(2,1)S(1)}, bf16[2,24,3456]{2,1,0:T(8,128)(2,1)S(1)}, u32[]{:S(2)}, u32[]{:S(2)}) collective-permute-start(bf16[2,24,3456]{2,1,0:T(8,128)(2,1)S(1)} %get-tuple-element.77), channel_id=1, source_target_pairs={{0,72},{8,64},{64,8},{72,0},{1,73},{9,65},{65,9},{73,1},{2,74},{10... | collective-permute-start | bytes 995336 | tf_op jit(solution)/shard_map/ppermute | solution.py:65
  470.4 15.1 %collective-permute-start.51 = (bf16[2,24,3456]{2,1,0:T(8,128)(2,1)S(1)}, bf16[2,24,3456]{2,1,0:T(8,128)(2,1)S(1)}, u32[]{:S(2)}, u32[]{:S(2)}) collective-permute-start(bf16[2,24,3456]{2,1,0:T(8,128)(2,1)S(1)} %get-tuple-element.76), channel_id=1, source_target_pairs={{0,64},{64,0},{1,65},{65,1},{2,66},{66,2},{3,67},{67,3},{4,68},{68... | collective-permute-start | bytes 995336 | tf_op jit(solution)/shard_map/ppermute | solution.py:54
  (87 other events, 1728.9 us)
Sparse Core Ops, SparseCore 0:
  47.1 114.4 all-gather.1
  278.8 87.8 reduce-scatter.1
